TPU v7x, 1024 devices: a whole 8x8x8 slice. The times are simulated.
1024 devices in a mesh: dp: 8 (over x), expert: 64 (over z, y), mp: 2 (over core).
Axes of the slice: x: 8, y: 8, z: 8, core: 2. Of those that a mesh axis runs over, the one named last changes fastest.
Arguments:
- image_rows: bfloat16 [81920, 2048], P(('dp', 'expert', 'mp')), may hold values from -6 to 6
- image_counts: int32 [1024, 16], P(('dp', 'expert', 'mp')), may hold values from 1 to 8, 80 in all within a row
- image_owner: int32 [1024, 16], P(('dp', 'expert', 'mp')), may hold values from 0 to 15, each once within a row
- routes: int32 [131072, 2], P(('dp', 'expert', 'mp')), may hold values from 0 to 63, all different within a row; in each aligned block of 128 rows (0 to 127, 128 to 255, ...) at most 6 rows name the same one
- route_scale: float32 [131072, 2], P(('dp', 'expert', 'mp')), may hold values from 0.1 to 1
- w_gate: bfloat16 [64, 2048, 768], P('expert', None, 'mp'), may hold values from -0.125 to 0.125
- w_up: bfloat16 [64, 2048, 768], P('expert', None, 'mp'), may hold values from -0.125 to 0.125
- w_down: bfloat16 [64, 768, 2048], P('expert', 'mp'), may hold values from -0.21875 to 0.21875
Outputs:
- combined: bfloat16 [131072, 2048], P(('dp', 'expert', 'mp'))
Inputs may be any that keep to these rules, and one draw needn't show every extreme that they name: `image_counts`: the counts of each device's images sum to 80, and each count is at most 8, reached on every device. `image_owner`: each device places its 16 images at distinct owners, one each. `routes`: a row's 2 experts are distinct; among the 128 rows of one device no expert is named more than 6 times, and this most is reached on some devices.
All inputs are finite; a program needn't handle non-finite values.
Results may differ from a plain program's by a relative error of at most 0.012.
Values may be sent and summed in bfloat16 or wider, within the bound.
No kernel may reach another device: no remote copies, remote signals or barrier semaphores. Data moves between devices by JAX's collectives and lax.ppermute only.
A program may use at most 64 MiB of HBM per device.

v0:
```python
import jax
import jax.numpy as jnp
from jax import lax
from jax.sharding import PartitionSpec as P


def local(image_rows, image_counts, image_owner, routes, route_scale, w_gate, w_up, w_down):
    owners = lax.axis_size(("dp", "mp"))
    length = routes.shape[0]
    fanout = routes.shape[1]
    width = image_rows.shape[1]
    slot_rows = length // owners
    counts = image_counts[0]
    placed = image_owner[0]
    owner_ids = jnp.arange(owners, dtype=jnp.int32)
    placed_at = placed[None, :] == owner_ids[:, None]
    starts = jnp.cumsum(counts) - counts
    count_to = jnp.sum(jnp.where(placed_at, counts[None, :], 0), axis=1)
    start_to = jnp.sum(jnp.where(placed_at, starts[None, :], 0), axis=1)
    within = jnp.arange(slot_rows, dtype=jnp.int32)
    row_index = jnp.clip(start_to[:, None] + within[None, :], 0, image_rows.shape[0] - 1)
    inside = within[None, :] < count_to[:, None]
    outgoing = jnp.where(inside[:, :, None], image_rows[row_index], jnp.zeros((), image_rows.dtype))
    arrived = lax.all_to_all(outgoing, ("dp", "mp"), split_axis=0, concat_axis=0, tiled=True)
    sequence = arrived.reshape(length, width)
    experts = lax.axis_size("expert")
    capacity = min(length, 3 * length * fanout // (2 * experts))
    pair_count = length * fanout
    flat_routes = routes.reshape(pair_count)
    onehot = (flat_routes[:, None] == jnp.arange(experts, dtype=jnp.int32)[None, :]).astype(
        jnp.int32
    )
    position = jnp.sum((jnp.cumsum(onehot, axis=0) - onehot) * onehot, axis=1)
    slot_id = flat_routes * capacity + position
    source_token = jnp.arange(pair_count, dtype=jnp.int32) // fanout
    buffer = (
        jnp.zeros((experts * capacity, width), jnp.bfloat16).at[slot_id].set(sequence[source_token])
    )
    received = lax.all_to_all(
        buffer.reshape(experts, capacity, width), "expert", split_axis=0, concat_axis=0, tiled=True
    )
    received = received.reshape(experts * capacity, width)
    gathered = lax.all_gather(received, "mp", axis=0, tiled=True)
    gate_sum = jnp.dot(gathered, w_gate[0], preferred_element_type=jnp.float32)
    up_sum = jnp.dot(gathered, w_up[0], preferred_element_type=jnp.float32)
    activated = (jax.nn.silu(gate_sum) * up_sum).astype(jnp.bfloat16)
    partial_out = jnp.dot(activated, w_down[0], preferred_element_type=jnp.float32).astype(
        jnp.bfloat16
    )
    result = lax.psum_scatter(partial_out, "mp", scatter_dimension=0, tiled=True).astype(
        jnp.float32
    )
    expert_out = result.astype(jnp.bfloat16)
    returned = lax.all_to_all(
        expert_out.reshape(experts, capacity, width),
        "expert",
        split_axis=0,
        concat_axis=0,
        tiled=True,
    )
    returned = returned.reshape(experts * capacity, width)
    picked = returned[slot_id].reshape(length, fanout, width).astype(jnp.float32)
    weights_norm = route_scale / jnp.sum(route_scale, axis=1, keepdims=True)
    combined = jnp.einsum("tr,trd->td", weights_norm, picked)
    return combined.astype(jnp.bfloat16)


def solution(mesh):
    return jax.shard_map(
        local,
        mesh=mesh,
        in_specs=(
            P(("dp", "expert", "mp"), None),
            P(("dp", "expert", "mp"), None),
            P(("dp", "expert", "mp"), None),
            P(("dp", "expert", "mp"), None),
            P(("dp", "expert", "mp"), None),
            P("expert", None, "mp"),
            P("expert", None, "mp"),
            P("expert", "mp", None),
        ),
        out_specs=P(("dp", "expert", "mp"), None),
        check_vma=False,
    )
```

profile of v0, /device:TPU:2, one launch (start us, length us, event | category | flops | bytes accessed | tf_op | source)
XLA Modules:
  0.0 266.6 jit_solution(15653148822989898079)
XLA Ops:
  6.5 0.0 copy-start
  6.5 1.0 reduce-window_2_clone.1
  7.5 0.7 subtract_bitcast_fusion
  8.2 0.8 select_reduce_fusion.1
  8.9 0.1 compare_select_fusion
  9.0 0.1 reshape.187
  9.1 0.1 iota_compare_fusion.3
  9.2 2.5 gather_fusion
  11.7 0.0 copy-start.2
  11.7 0.9 bitcast_select_fusion
  12.6 16.6 %all-to-all-start = ((bf16[16,8,2048]{2,1,0:T(8,128)(2,1)}), bf16[16,8,2048]{2,1,0:T(8,128)(2,1)S(1)}, u32[]{:S(2)}, u32[]{:S(2)}) async-start(bf16[16,8,2048]{2,1,0:T(8,128)(2,1)} %bitcast_select_fusion), calls=%async_computation | async-start | bytes 1048576 | tf_op jit(solution)/shard_map/all_to_all | solution.py:24
  29.1 0.0 all-gather.2.cloned.1.call-start
  29.2 0.0 copy-done.2
  29.2 0.1 copy.14
  29.3 0.1 eq.44
  29.5 0.1 eq.40
  29.6 0.6 reduce-window.9
  30.2 0.2 slice_reduce_fusion
  30.4 0.1 copy.13
  30.6 0.1 mul.28
  30.7 0.1 fusion.19
  30.8 12.6 %all-to-all-done = bf16[16,8,2048]{2,1,0:T(8,128)(2,1)S(1)} async-done(((bf16[16,8,2048]{2,1,0:T(8,128)(2,1)}), bf16[16,8,2048]{2,1,0:T(8,128)(2,1)S(1)}, u32[]{:S(2)}, u32[]{:S(2)}) %all-to-all-start) | async-done | bytes 524320 | tf_op jit(solution)/shard_map/all_to_all | solution.py:24
  43.5 0.0 copy-start.1
  43.5 0.8 copy-done.1
  44.3 6.0 %scatter_custom_fusion = bf16[384,2048]{1,0:T(8,128)(2,1)S(1)} fusion(s32[256]{0:T(256)S(1)} %bitcast.57, bf16[128,2048]{1,0:T(8,128)(2,1)} %bitcast.55, s32[1024]{0:T(1024)S(1)} %pad_clamp_fusion.1, bf16[]{:T(256)} %constant.34.clone.1), kind=kCustom, calls=%fused_computation.13 | custom fusion | bytes 1573376 | tf_op jit(solution)/shard_map/scatter | solution.py:37
  50.3 1.6 reshape.180
  51.8 67.2 %all_to_all.15 = bf16[64,6,2048]{2,1,0:T(8,128)(2,1)} all-to-all(bf16[64,6,2048]{2,1,0:T(8,128)(2,1)} %reshape.180), channel_id=1, replica_groups=mesh['dp'=8,'expert'=64,'mp'=2] {'expert'}, dimensions={0} | all-to-all | bytes 3145728 | tf_op jit(solution)/shard_map/all_to_all | solution.py:39
  119.1 3.7 %reshape.181 = bf16[384,2048]{1,0:T(8,128)(2,1)} reshape(bf16[64,6,2048]{2,1,0:T(8,128)(2,1)} %all_to_all.15) | data formatting | bytes 3145728 | tf_op jit(solution)/shard_map/reshape | solution.py:42
  122.8 0.0 copy-start.4
  122.8 0.0 all-gather.2.cloned.1.call-update
  122.8 0.2 reduce-scatter.2.cloned.1.call-start
  123.0 20.1 %all-gather.2.cloned.1.call-done = bf16[768,2048]{1,0:T(8,128)(2,1)} async-done(((bf16[384,2048]{1,0:T(8,128)(2,1)}), bf16[768,2048]{1,0:T(8,128)(2,1)}) %all-gather.2.cloned.1.call-update) | async-done | bytes 3145744 | tf_op jit(solution)/shard_map/all_gather | solution.py:43
  143.1 0.0 copy-done.4
  143.1 4.7 %fusion.3 = f32[768,384]{1,0:T(8,128)} fusion(bf16[768,2048]{1,0:T(8,128)(2,1)} %all-gather.2.cloned.1.call-done, bf16[1,2048,384]{2,1,0:T(8,128)(2,1)S(1)} %copy-done.4), kind=kOutput, calls=%fused_computation.8 | convolution fusion | flops 1207959552 | bytes 5898240 | tf_op jit(solution)/shard_map/dot_general | solution.py:44
  147.8 0.0 copy-done
  147.8 7.8 %convolution_convert_fusion = bf16[768,2048]{1,0:T(8,128)(2,1)} fusion(bf16[1,384,2048]{2,1,0:T(8,128)(2,1)S(1)} %copy-done, bf16[768,2048]{1,0:T(8,128)(2,1)} %all-gather.2.cloned.1.call-done, bf16[1,2048,384]{2,1,0:T(8,128)(2,1)} %param.14, f32[768,384]{1,0:T(8,128)} %fusion.3), kind=kOutput, calls=%fused_computation.4 | convolution fusion | flops 2419261440 | bytes 10616832 | tf_op jit(solution)/shard_map/dot_general | solution.py:47
  155.6 0.0 reduce-scatter.2.cloned.1.call-update
  155.7 23.7 %reduce-scatter.2.cloned.1.call-done = bf16[384,2048]{1,0:T(8,128)(2,1)} async-done(((bf16[768,2048]{1,0:T(8,128)(2,1)}), bf16[384,2048]{1,0:T(8,128)(2,1)}) %reduce-scatter.2.cloned.1.call-update) | async-done | bytes 1572880 | tf_op jit(solution)/shard_map/reduce_scatter | solution.py:50
  179.4 3.7 %reshape.182 = bf16[64,6,2048]{2,1,0:T(8,128)(2,1)} reshape(bf16[384,2048]{1,0:T(8,128)(2,1)} %reduce-scatter.2.cloned.1.call-done) | data formatting | bytes 3145728 | tf_op jit(solution)/shard_map/reshape | solution.py:55
  183.1 14.5 %all-to-all-start.2 = ((bf16[64,6,2048]{2,1,0:T(8,128)(2,1)}), bf16[64,6,2048]{2,1,0:T(8,128)(2,1)}, u32[]{:S(2)}, u32[]{:S(2)}) async-start(bf16[64,6,2048]{2,1,0:T(8,128)(2,1)} %reshape.182), calls=%async_computation.3 | async-start | bytes 4194304 | tf_op jit(solution)/shard_map/all_to_all | solution.py:54
  197.6 0.0 copy-done.3
  197.6 0.1 copy.17
  197.8 52.9 %all-to-all-done.2 = bf16[64,6,2048]{2,1,0:T(8,128)(2,1)} async-done(((bf16[64,6,2048]{2,1,0:T(8,128)(2,1)}), bf16[64,6,2048]{2,1,0:T(8,128)(2,1)}, u32[]{:S(2)}, u32[]{:S(2)}) %all-to-all-start.2) | async-done | bytes 1572896 | tf_op jit(solution)/shard_map/all_to_all | solution.py:54
  250.7 2.6 reshape.183
  253.3 2.3 gather_fusion.1
  255.7 1.7 reshape.184
  257.4 1.2 fusion.22
  258.7 1.1 copy.22
  (12 shorter events, 0.1 us)
Async XLA Ops:
  6.5 141.3 %copy-start = (bf16[1,384,2048]{2,1,0:T(8,128)(2,1)S(1)}, bf16[1,384,2048]{2,1,0:T(8,128)(2,1)}, u32[]{:S(2)}) copy-start(bf16[1,384,2048]{2,1,0:T(8,128)(2,1)} %param.15) | copy-start | bytes 4718596
  11.7 17.5 %copy-start.2 = (s32[128,2]{0,1:T(2,128)S(1)}, s32[128,2]{0,1:T(2,128)}, u32[]{:S(2)}) copy-start(s32[128,2]{0,1:T(2,128)} %param.11) | copy-start | bytes 3076
  12.6 30.9 %all-to-all-start = ((bf16[16,8,2048]{2,1,0:T(8,128)(2,1)}), bf16[16,8,2048]{2,1,0:T(8,128)(2,1)S(1)}, u32[]{:S(2)}, u32[]{:S(2)}) async-start(bf16[16,8,2048]{2,1,0:T(8,128)(2,1)} %bitcast_select_fusion), calls=%async_computation | async-start | bytes 1048576 | tf_op jit(solution)/shard_map/all_to_all | solution.py:24
  29.1 114.0 %all-gather.2.cloned.1.call-start = ((), (), s32[]{:S(2)}) async-start(), calls=%async_computation.4 | async-start | bytes 4718592 | tf_op jit(solution)/shard_map/all_gather | solution.py:43
  43.5 0.8 copy-start.1
  122.8 20.3 %copy-start.4 = (bf16[1,2048,384]{2,1,0:T(8,128)(2,1)S(1)}, bf16[1,2048,384]{2,1,0:T(8,128)(2,1)}, u32[]{:S(2)}) copy-start(bf16[1,2048,384]{2,1,0:T(8,128)(2,1)} %param.13) | copy-start | bytes 4718596
  122.8 56.6 %reduce-scatter.2.cloned.1.call-start = ((), (), s32[]{:S(2)}) async-start(), calls=%async_computation.5 | async-start | bytes 4718592 | tf_op jit(solution)/shard_map/reduce_scatter | solution.py:50
  183.1 14.5 %copy-start.3 = (f32[128,2]{0,1:T(2,128)S(1)}, f32[128,2]{0,1:T(2,128)}, u32[]{:S(2)}) copy-start(f32[128,2]{0,1:T(2,128)} %param.12) | copy-start | bytes 3076
  183.1 67.7 %all-to-all-start.2 = ((bf16[64,6,2048]{2,1,0:T(8,128)(2,1)}), bf16[64,6,2048]{2,1,0:T(8,128)(2,1)}, u32[]{:S(2)}, u32[]{:S(2)}) async-start(bf16[64,6,2048]{2,1,0:T(8,128)(2,1)} %reshape.182), calls=%async_computation.3 | async-start | bytes 4194304 | tf_op jit(solution)/shard_map/all_to_all | solution.py:54
Sparse Core Ops, SparseCore 0:
  122.9 20.1 all-gather.1
  155.8 23.5 reduce-scatter.1
where the time goes:
time: 267 us
  waiting for transfers between devices  109 us (41%)
  blocking collectives  67.2 us (25%)
  starting transfers between devices  31.3 us (12%)
  local copies, waits for them, and re-layouts  27.1 us (10%)
  matrix products  13.8 us (5%)
  between operations  13.6 us (5%)
  other arithmetic  4.27 us (2%)
    all_to_all x1, blocking collectives, local(): lax.all_to_all(buffer.reshape(experts, capacity, width), 'expert', split_...  67.2 us
    all_to_all x1, waiting for transfers between devices, local(): lax.all_to_all(expert_out.reshape(experts, capacity, width), 'expert', sp...  52.9 us
    reduce_scatter x1, waiting for transfers between devices, local(): lax.psum_scatter(partial_out, 'mp', scatter_dimension=0, tiled=True)  23.7 us
    all_gather x1, waiting for transfers between devices, local(): gathered = lax.all_gather(received, 'mp', axis=0, tiled=True)  20.1 us
    all_to_all x1, starting transfers between devices, local(): lax.all_to_all(outgoing, ('dp', 'mp'), split_axis=0, concat_axis=0, tiled...  16.6 us
    all_to_all x1, starting transfers between devices, local(): lax.all_to_all(expert_out.reshape(experts, capacity, width), 'expert', sp...  14.5 us
    all_to_all x1, waiting for transfers between devices, local(): lax.all_to_all(outgoing, ('dp', 'mp'), split_axis=0, concat_axis=0, tiled...  12.6 us
    dot_general x1, matrix products, local(): jnp.dot(activated, w_down[0], preferred_element_type=jnp.float32)  7.82 us
  transfers between devices with their start and end apart: 4, of which 4 were waited for; matrix products, arithmetic and copies ran while one was open for 1% of the time, Pallas kernels for 0%

commit v1 on v0

v1 whole, which is shorter than its diff:
```python
import jax
import jax.numpy as jnp
from jax import lax
from jax.experimental import pallas as pl
from jax.experimental.pallas import tpu as pltpu
from jax.sharding import PartitionSpec as P

BF16 = jnp.bfloat16
F32 = jnp.float32
I32 = jnp.int32
VMEM = pl.BlockSpec(memory_space=pltpu.VMEM)

CAP = 6
GROUP = 8
BLOCKS = 3


def iota(shape, dim):
    return lax.broadcasted_iota(I32, shape, dim)


def dot(a, b):
    return jnp.dot(a, b, preferred_element_type=F32)


def pack_kernel(counts_ref, owner_ref, rows_ref, out_ref):
    images = counts_ref.shape[1]
    length, slot = out_ref.shape[0], out_ref.shape[0] // images
    counts = counts_ref[...]
    row = iota((length, images), 0)
    image = iota((length, images), 1)
    placed = owner_ref[...] == row // slot
    count = jnp.sum(jnp.where(placed, counts, 0), axis=1, keepdims=True)
    index = jnp.sum(jnp.where(placed, image, 0), axis=1, keepdims=True)
    start = jnp.sum(jnp.where(image < index, counts, 0), axis=1, keepdims=True)
    within = iota((length, 1), 0) % slot
    source = jnp.where(within < count, start + within, -1)
    pick = (iota((length, rows_ref.shape[0]), 1) == source).astype(F32).astype(BF16)
    out_ref[...] = dot(pick, rows_ref[...]).astype(BF16)


def dispatch_kernel(routes_ref, rows_ref, out_ref):
    length, width = rows_ref.shape
    experts = out_ref.shape[0] // GROUP
    block = width // (BLOCKS + 1)
    expert = iota((experts, length), 0)
    named = (expert == routes_ref[0:1, :]) | (expert == routes_ref[1:2, :])
    earlier = (iota((length, length), 0) < iota((length, length), 1)).astype(F32).astype(BF16)
    position = dot(named.astype(F32).astype(BF16), earlier)
    position = jnp.where(named, position, -1.0)[:, None, :]
    k = iota((experts, GROUP, length), 1)

    def placed(wanted):
        hit = position == wanted.astype(F32)
        return hit.astype(F32).reshape(experts * GROUP, length).astype(BF16)

    main = placed(jnp.where(k < CAP, k, -2))
    tail_rows = rows_ref[:, BLOCKS * block :]
    for j in range(BLOCKS):
        tail = placed(jnp.where(k == CAP, j, jnp.where(k == CAP + 1, BLOCKS + j, -2)))
        both = jnp.concatenate([main, tail], axis=1)
        source = jnp.concatenate([rows_ref[:, j * block : (j + 1) * block], tail_rows], axis=0)
        out_ref[:, j * block : (j + 1) * block] = dot(both, source).astype(BF16)


def expert_kernel(x_ref, gate_a, up_a, down_a, gate_b, up_b, down_b, out_ref, tail_ref, act_ref):
    rows, wide = x_ref.shape
    block = wide // BLOCKS
    half = gate_a.shape[1]
    step = 128
    r = iota((step, step), 0)
    c = iota((step, step), 1)
    same = r // GROUP == c // GROUP
    k_r, k_c = r % GROUP, c % GROUP

    def onehot(mask):
        return (same & mask).astype(F32).astype(BF16)

    gather = jnp.concatenate(
        [
            onehot(((k_r == j) & (k_c == CAP)) | ((k_r == BLOCKS + j) & (k_c == CAP + 1)))
            for j in range(BLOCKS)
        ],
        axis=1,
    )
    for g in range(rows // step):
        at = slice(g * step, (g + 1) * step)
        stacked = jnp.concatenate(
            [x_ref[at, j * block : (j + 1) * block] for j in range(BLOCKS)], axis=0
        )
        tail_ref[at, :] = dot(gather, stacked).astype(BF16)

    for at, gate_ref, up_ref in ((0, gate_a, up_a), (half, gate_b, up_b)):
        gate = dot(x_ref[...], gate_ref[:wide, :]) + dot(tail_ref[...], gate_ref[wide:, :])
        up = dot(x_ref[...], up_ref[:wide, :]) + dot(tail_ref[...], up_ref[wide:, :])
        act_ref[:, at : at + half] = (gate / (1.0 + jnp.exp(-gate)) * up).astype(BF16)

    def down(at):
        return dot(act_ref[:, :half], down_a[:, at : at + block]) + dot(
            act_ref[:, half:], down_b[:, at : at + block]
        )

    tail_ref[...] = down(wide).astype(BF16)
    is_slot = iota((step, block), 0) % GROUP < CAP
    for j in range(BLOCKS):
        spread = onehot(((k_c == j) & (k_r == CAP)) | ((k_c == BLOCKS + j) & (k_r == CAP + 1)))
        main = down(j * block)
        for g in range(rows // step):
            at = slice(g * step, (g + 1) * step)
            moved = dot(spread, tail_ref[at, :])
            out_ref[at, j * block : (j + 1) * block] = jnp.where(is_slot, main[at, :], moved).astype(
                BF16
            )


def combine_kernel(routes_ref, scale_ref, back_ref, out_ref):
    length = routes_ref.shape[0]
    slots = back_ref.shape[0]
    experts = slots // GROUP
    block = back_ref.shape[1] // BLOCKS
    scale = scale_ref[...]
    share = scale / jnp.sum(scale, axis=1, keepdims=True)
    expert = iota((length, experts), 1)
    hits = [expert == routes_ref[:, r : r + 1] for r in range(2)]
    named = (hits[0] | hits[1]).astype(F32).astype(BF16)
    earlier = (iota((length, length), 1) < iota((length, length), 0)).astype(F32).astype(BF16)
    position = dot(earlier, named)
    slot = iota((length, slots), 1)
    at = []
    for r in range(2):
        k = jnp.sum(jnp.where(hits[r], position, 0.0), axis=1, keepdims=True).astype(I32)
        at.append((k, routes_ref[:, r : r + 1] * GROUP))

    def onehot(index):
        return (slot == index).astype(F32).astype(BF16)

    main = [onehot(base + k) for k, base in at]
    tails = [jnp.zeros((length, block), F32) for _ in range(2)]
    for j in range(BLOCKS):
        picks = list(main)
        for k, base in at:
            second = k >= BLOCKS
            mine = jnp.where(second, k - BLOCKS, k) == j
            picks.append(onehot(jnp.where(mine, base + CAP + second.astype(I32), -1)))
        got = dot(jnp.concatenate(picks, axis=0), back_ref[:, j * block : (j + 1) * block])
        total = share[:, 0:1] * got[:length] + share[:, 1:2] * got[length : 2 * length]
        out_ref[:, j * block : (j + 1) * block] = total.astype(BF16)
        for r in range(2):
            tails[r] = tails[r] + got[(2 + r) * length : (3 + r) * length]
    total = share[:, 0:1] * tails[0] + share[:, 1:2] * tails[1]
    out_ref[:, BLOCKS * block :] = total.astype(BF16)


def call(kernel, out, *args, flops, scratch=(), limit=32 << 20):
    moved = sum(a.size * a.dtype.itemsize for a in args) + out[0] * out[1] * 2
    return pl.pallas_call(
        kernel,
        out_shape=jax.ShapeDtypeStruct(out, BF16),
        in_specs=[VMEM] * len(args),
        out_specs=VMEM,
        scratch_shapes=list(scratch),
        compiler_params=pltpu.CompilerParams(vmem_limit_bytes=limit),
        cost_estimate=pl.CostEstimate(flops=flops, bytes_accessed=moved, transcendentals=0),
    )(*args)


def local(image_rows, image_counts, image_owner, routes, route_scale, w_gate, w_up, w_down):
    owners = lax.axis_size(("dp", "mp"))
    experts = lax.axis_size("expert")
    length = routes.shape[0]
    width = image_rows.shape[1]
    slots = experts * GROUP
    wide = width // (BLOCKS + 1) * BLOCKS
    own = [w_gate[0], w_up[0], w_down[0]]
    half = own[0].shape[1]
    other = [lax.ppermute(w, "mp", [(0, 1), (1, 0)]) for w in own]

    outgoing = call(
        pack_kernel,
        (length, width),
        image_counts,
        image_owner,
        image_rows,
        flops=2 * length * image_rows.shape[0] * width,
    )
    arrived = lax.all_to_all(
        outgoing.reshape(owners, length // owners, width),
        ("dp", "mp"),
        split_axis=0,
        concat_axis=0,
        tiled=True,
    )
    sequence = arrived.reshape(length, width)
    buffer = call(
        dispatch_kernel, (slots, wide), routes.T, sequence, flops=4 * slots * length * wide
    )

    def exchange(x):
        y = lax.all_to_all(
            x.reshape(experts, GROUP, wide), "expert", split_axis=0, concat_axis=0, tiled=True
        )
        return y.reshape(slots, wide)

    received = exchange(buffer)
    result = call(
        expert_kernel,
        (slots, wide),
        received,
        *own,
        *other,
        flops=12 * slots * width * half,
        scratch=[pltpu.VMEM((slots, wide // BLOCKS), BF16), pltpu.VMEM((slots, 2 * half), BF16)],
    )
    returned = exchange(result)
    return call(
        combine_kernel,
        (length, width),
        routes,
        route_scale,
        returned,
        flops=8 * length * slots * wide,
    )


def solution(mesh):
    return jax.shard_map(
        local,
        mesh=mesh,
        in_specs=(
            P(("dp", "expert", "mp"), None),
            P(("dp", "expert", "mp"), None),
            P(("dp", "expert", "mp"), None),
            P(("dp", "expert", "mp"), None),
            P(("dp", "expert", "mp"), None),
            P("expert", None, "mp"),
            P("expert", None, "mp"),
            P("expert", "mp", None),
        ),
        out_specs=P(("dp", "expert", "mp"), None),
        check_vma=False,
    )
```

time: 267 us -> 162 us (0.61)
  the two profiles are of different devices: /device:TPU:2 before, /device:TPU:16 now
where the time goes in v1:
time: 162 us; the launch traced here: 161 us
  waiting for transfers between devices  72.3 us (45%)
  starting transfers between devices  39.5 us (24%)
  blocking collectives  22.7 us (14%)
  Pallas kernels  13.2 us (8%)
  local copies, waits for them, and re-layouts  13 us (8%)
    all_to_all x2, waiting for transfers between devices, exchange(): lax.all_to_all(x.reshape(experts, GROUP, wide), 'expert', split_axis=0, c...  71.2 us
    all_to_all x2, starting transfers between devices, exchange(): lax.all_to_all(x.reshape(experts, GROUP, wide), 'expert', split_axis=0, c...  32.1 us
    all_to_all x1, blocking collectives, local(): lax.all_to_all(outgoing.reshape(owners, length // owners, width), ('dp',...  22.7 us
    pallas_call x4, Pallas kernels, call(): pl.pallas_call(kernel, out_shape=jax.ShapeDtypeStruct(out, BF16), in_spec...  13.2 us
    unnamed x30, local copies, waits for them, and re-layouts  13 us
    ppermute x3, starting transfers between devices, local(): other = [lax.ppermute(w, 'mp', [(0, 1), (1, 0)]) for w in own]  7.38 us
  transfers between devices with their start and end apart: 5, of which 3 were waited for; matrix products, arithmetic and copies ran while one was open for 0% of the time, Pallas kernels for 0%

profile of v1, /device:TPU:16, one launch (start us, length us, event | category | flops | bytes accessed | tf_op | source)
XLA Modules:
  0.0 160.9 jit_solution(5955427733078426048)
XLA Ops:
  0.0 0.0 copy-start
  0.0 1.0 copy-done
  1.0 0.0 copy-start.2
  1.0 0.7 copy-done.2
  1.6 0.0 copy-start.3
  1.6 0.7 copy-done.3
  2.3 0.0 copy-start.1
  2.3 0.5 shard_map.82
  2.7 22.7 %all_to_all.15 = bf16[16,8,2048]{2,1,0:T(8,128)(2,1)S(1)} all-to-all(bf16[16,8,2048]{2,1,0:T(8,128)(2,1)S(1)} %bitcast.10), channel_id=1, replica_groups=mesh['dp'=8,'expert'=64,'mp'=2] {'dp','mp'}, dimensions={0} | all-to-all | bytes 1048576 | tf_op jit(solution)/shard_map/all_to_all | solution.py:186
  25.4 0.0 copy-done.1
  25.4 1.9 %shard_map.83 = bf16[512,1536]{1,0:T(8,128)(2,1)} custom-call(s32[2,128]{1,0:T(2,128)S(1)} %bitcast.14, bf16[128,2048]{1,0:T(8,128)(2,1)S(1)} %bitcast.11), custom_call_target="tpu_custom_call" | custom-call | flops 402653184 | bytes 2098176 | tf_op jit(solution)/shard_map/pallas_call | solution.py:156
  27.3 0.0 copy-start.4
  27.3 23.4 %all-to-all-start.1 = ((bf16[64,8,1536]{2,1,0:T(8,128)(2,1)}), bf16[64,8,1536]{2,1,0:T(8,128)(2,1)S(1)}, u32[]{:S(2)}, u32[]{:S(2)}) async-start(bf16[64,8,1536]{2,1,0:T(8,128)(2,1)} %bitcast.3), calls=%async_computation.1 | async-start | bytes 3145728 | tf_op jit(solution)/shard_map/all_to_all | solution.py:199
  50.8 0.0 copy-done.4
  50.8 3.1 %collective-permute-start = (bf16[2048,384]{1,0:T(8,128)(2,1)S(1)}, bf16[2048,384]{1,0:T(8,128)(2,1)S(1)}, u32[]{:S(2)}, u32[]{:S(2)}) collective-permute-start(bf16[2048,384]{1,0:T(8,128)(2,1)S(1)} %bitcast.15), channel_id=1, source_target_pairs={{0,1},{1,0},{2,3},{3,2},{4,5},{5,4},{6,7},{7,6},{8,9},{9,8},{10,11... | collective-permute-start | bytes 4718600 | tf_op jit(solution)/shard_map/ppermute | solution.py:176
  53.8 1.9 %collective-permute-start.1 = (bf16[2048,384]{1,0:T(8,128)(2,1)}, bf16[2048,384]{1,0:T(8,128)(2,1)S(1)}, u32[]{:S(2)}, u32[]{:S(2)}) collective-permute-start(bf16[2048,384]{1,0:T(8,128)(2,1)} %bitcast.17), channel_id=1, source_target_pairs={{0,1},{1,0},{2,3},{3,2},{4,5},{5,4},{6,7},{7,6},{8,9},{9,8},{10,11... | collective-permute-start | bytes 4718600 | tf_op jit(solution)/shard_map/ppermute | solution.py:176
  55.8 2.4 %collective-permute-start.2 = (bf16[384,2048]{1,0:T(8,128)(2,1)}, bf16[384,2048]{1,0:T(8,128)(2,1)S(1)}, u32[]{:S(2)}, u32[]{:S(2)}) collective-permute-start(bf16[384,2048]{1,0:T(8,128)(2,1)} %bitcast.19), channel_id=1, source_target_pairs={{0,1},{1,0},{2,3},{3,2},{4,5},{5,4},{6,7},{7,6},{8,9},{9,8},{10,11... | collective-permute-start | bytes 4718600 | tf_op jit(solution)/shard_map/ppermute | solution.py:176
  58.2 0.0 collective-permute-done.gate_b
  58.2 0.0 copy-start.7
  58.2 1.1 copy-done.7
  59.3 0.0 collective-permute-done.1.up_b
  59.3 0.0 copy-start.9
  59.3 1.2 copy-done.9
  60.5 1.1 collective-permute-done.2.down_b
  61.6 0.0 copy-start.11
  61.6 1.2 copy-done.11
  62.8 29.5 %all-to-all-done.1 = bf16[64,8,1536]{2,1,0:T(8,128)(2,1)S(1)} async-done(((bf16[64,8,1536]{2,1,0:T(8,128)(2,1)}), bf16[64,8,1536]{2,1,0:T(8,128)(2,1)S(1)}, u32[]{:S(2)}, u32[]{:S(2)}) %all-to-all-start.1) | async-done | bytes 1572896 | tf_op jit(solution)/shard_map/all_to_all | solution.py:199
  92.3 0.0 copy-start.5
  92.3 1.4 copy-done.5
  93.7 0.0 copy-start.6
  93.7 1.4 copy-done.6
  95.2 0.0 copy-start.8
  95.2 1.4 copy-done.8
  96.6 0.0 copy-start.10
  96.6 1.4 copy-done.10
  98.0 0.0 copy-start.12
  98.0 1.4 copy-done.12
  99.4 8.6 %shard_map.84 = bf16[512,1536]{1,0:T(8,128)(2,1)} custom-call(bf16[512,1536]{1,0:T(8,128)(2,1)S(1)} %bitcast.12, bf16[2048,384]{1,0:T(8,128)(2,1)S(1)} %bitcast.16, bf16[2048,384]{1,0:T(8,128)(2,1)S(1)} %bitcast.18, bf16[384,2048]{1,0:T(8,128)(2,1)S(1)} %bitcast.20, bf16[2048,384]{1,0:T(8,128)(2,1)S(1)} %copy-done.8, bf16[2048,384]{1,0:T(8,128)(2,1)S(1)} %copy-done.10, ...), custom_call_target="tpu_custom_call" | custom-call | flops 4831838208 | bytes 12582912 | tf_op jit(solution)/shard_map/pallas_call | solution.py:156
  108.0 0.0 copy-start.13
  108.0 8.7 %all-to-all-start.2 = ((bf16[64,8,1536]{2,1,0:T(8,128)(2,1)}), bf16[64,8,1536]{2,1,0:T(8,128)(2,1)S(1)}, u32[]{:S(2)}, u32[]{:S(2)}) async-start(bf16[64,8,1536]{2,1,0:T(8,128)(2,1)} %bitcast.8), calls=%async_computation.2 | async-start | bytes 3145728 | tf_op jit(solution)/shard_map/all_to_all | solution.py:199
  116.7 0.1 copy.9.routes_ref
  116.8 0.0 copy-done.13
  116.8 0.1 copy.10.scale_ref
  116.9 41.7 %all-to-all-done.2 = bf16[64,8,1536]{2,1,0:T(8,128)(2,1)S(1)} async-done(((bf16[64,8,1536]{2,1,0:T(8,128)(2,1)}), bf16[64,8,1536]{2,1,0:T(8,128)(2,1)S(1)}, u32[]{:S(2)}, u32[]{:S(2)}) %all-to-all-start.2) | async-done | bytes 1572896 | tf_op jit(solution)/shard_map/all_to_all | solution.py:199
  158.6 2.3 %shard_map.85 = bf16[128,2048]{1,0:T(8,128)(2,1)} custom-call(s32[128,2]{1,0:T(8,128)S(1)} %copy.9.routes_ref, f32[128,2]{1,0:T(8,128)S(1)} %copy.10.scale_ref, bf16[512,1536]{1,0:T(8,128)(2,1)S(1)} %bitcast.13), custom_call_target="tpu_custom_call" | custom-call | flops 805306368 | bytes 2099200 | tf_op jit(solution)/shard_map/pallas_call | solution.py:156
Async XLA Ops:
  0.0 1.0 copy-start
  1.0 0.7 copy-start.2
  1.6 0.7 copy-start.3
  2.3 23.2 %copy-start.1 = (s32[128,2]{0,1:T(2,128)S(1)}, s32[128,2]{0,1:T(2,128)}, u32[]{:S(2)}) copy-start(s32[128,2]{0,1:T(2,128)} %param.11) | copy-start | bytes 3076
  27.3 23.4 %copy-start.4 = (bf16[1,2048,384]{2,1,0:T(8,128)(2,1)S(1)}, bf16[1,2048,384]{2,1,0:T(8,128)(2,1)}, u32[]{:S(2)}) copy-start(bf16[1,2048,384]{2,1,0:T(8,128)(2,1)} %param.13) | copy-start | bytes 4718596
  27.3 65.0 %all-to-all-start.1 = ((bf16[64,8,1536]{2,1,0:T(8,128)(2,1)}), bf16[64,8,1536]{2,1,0:T(8,128)(2,1)S(1)}, u32[]{:S(2)}, u32[]{:S(2)}) async-start(bf16[64,8,1536]{2,1,0:T(8,128)(2,1)} %bitcast.3), calls=%async_computation.1 | async-start | bytes 3145728 | tf_op jit(solution)/shard_map/all_to_all | solution.py:199
  50.8 7.4 %collective-permute-start = (bf16[2048,384]{1,0:T(8,128)(2,1)S(1)}, bf16[2048,384]{1,0:T(8,128)(2,1)S(1)}, u32[]{:S(2)}, u32[]{:S(2)}) collective-permute-start(bf16[2048,384]{1,0:T(8,128)(2,1)S(1)} %bitcast.15), channel_id=1, source_target_pairs={{0,1},{1,0},{2,3},{3,2},{4,5},{5,4},{6,7},{7,6},{8,9},{9,8},{10,11... | collective-permute-start | bytes 4718600 | tf_op jit(solution)/shard_map/ppermute | solution.py:176
  53.8 5.5 %collective-permute-start.1 = (bf16[2048,384]{1,0:T(8,128)(2,1)}, bf16[2048,384]{1,0:T(8,128)(2,1)S(1)}, u32[]{:S(2)}, u32[]{:S(2)}) collective-permute-start(bf16[2048,384]{1,0:T(8,128)(2,1)} %bitcast.17), channel_id=1, source_target_pairs={{0,1},{1,0},{2,3},{3,2},{4,5},{5,4},{6,7},{7,6},{8,9},{9,8},{10,11... | collective-permute-start | bytes 4718600 | tf_op jit(solution)/shard_map/ppermute | solution.py:176
  55.8 5.8 %collective-permute-start.2 = (bf16[384,2048]{1,0:T(8,128)(2,1)}, bf16[384,2048]{1,0:T(8,128)(2,1)S(1)}, u32[]{:S(2)}, u32[]{:S(2)}) collective-permute-start(bf16[384,2048]{1,0:T(8,128)(2,1)} %bitcast.19), channel_id=1, source_target_pairs={{0,1},{1,0},{2,3},{3,2},{4,5},{5,4},{6,7},{7,6},{8,9},{9,8},{10,11... | collective-permute-start | bytes 4718600 | tf_op jit(solution)/shard_map/ppermute | solution.py:176
  58.2 1.1 copy-start.7
  59.3 1.2 copy-start.9
  61.6 1.2 copy-start.11
  92.3 1.4 copy-start.5
  93.7 1.4 copy-start.6
  95.2 1.4 copy-start.8
  96.6 1.4 copy-start.10
  98.0 1.4 copy-start.12
  108.0 8.8 %copy-start.13 = (f32[128,2]{0,1:T(2,128)S(1)}, f32[128,2]{0,1:T(2,128)}, u32[]{:S(2)}) copy-start(f32[128,2]{0,1:T(2,128)} %param.12) | copy-start | bytes 3076
  108.0 50.6 %all-to-all-start.2 = ((bf16[64,8,1536]{2,1,0:T(8,128)(2,1)}), bf16[64,8,1536]{2,1,0:T(8,128)(2,1)S(1)}, u32[]{:S(2)}, u32[]{:S(2)}) async-start(bf16[64,8,1536]{2,1,0:T(8,128)(2,1)} %bitcast.8), calls=%async_computation.2 | async-start | bytes 3145728 | tf_op jit(solution)/shard_map/all_to_all | solution.py:199

commit v2 on v1

v2 whole, which is shorter than its diff:
```python
import jax
import jax.numpy as jnp
from jax import lax
from jax.experimental import pallas as pl
from jax.experimental.pallas import tpu as pltpu
from jax.sharding import PartitionSpec as P

BF16 = jnp.bfloat16
F32 = jnp.float32
I32 = jnp.int32
VMEM = pl.BlockSpec(memory_space=pltpu.VMEM)
ANY = pl.BlockSpec(memory_space=pl.ANY)

CAP = 6
GROUP = 8
BLOCKS = 3


def iota(shape, dim):
    return lax.broadcasted_iota(I32, shape, dim)


def dot(a, b):
    return jnp.dot(a, b, preferred_element_type=F32)


def start(*pairs):
    copies = [pltpu.make_async_copy(*pair) for pair in pairs]
    for copy in copies:
        copy.start()
    return copies


def finish(copies):
    for copy in copies:
        copy.wait()


def pack_kernel(
    counts_hbm, owner_hbm, rows_hbm, out_hbm, counts_ref, owner_ref, rows_ref, out_ref, sems
):
    small = start(
        (counts_hbm, counts_ref, sems.at[0]),
        (owner_hbm, owner_ref, sems.at[1]),
    )
    large = start((rows_hbm, rows_ref, sems.at[2]))
    finish(small)
    images = counts_ref.shape[1]
    length, slot = out_ref.shape[0], out_ref.shape[0] // images
    counts = counts_ref[...]
    row = iota((length, images), 0)
    image = iota((length, images), 1)
    placed = owner_ref[...] == row // slot
    count = jnp.sum(jnp.where(placed, counts, 0), axis=1, keepdims=True)
    index = jnp.sum(jnp.where(placed, image, 0), axis=1, keepdims=True)
    first = jnp.sum(jnp.where(image < index, counts, 0), axis=1, keepdims=True)
    within = iota((length, 1), 0) % slot
    source = jnp.where(within < count, first + within, -1)
    pick = (iota((length, rows_ref.shape[0]), 1) == source).astype(F32).astype(BF16)
    finish(large)
    out_ref[...] = dot(pick, rows_ref[...]).astype(BF16)
    finish(start((out_ref, out_hbm, sems.at[3])))


def dispatch_kernel(routes_ref, rows_ref, out_hbm, out_ref, sems):
    length, width = rows_ref.shape
    experts = out_ref.shape[0] // GROUP
    block = width // (BLOCKS + 1)
    expert = iota((experts, length), 0)
    named = (expert == routes_ref[0:1, :]) | (expert == routes_ref[1:2, :])
    earlier = (iota((length, length), 0) < iota((length, length), 1)).astype(F32).astype(BF16)
    position = dot(named.astype(F32).astype(BF16), earlier)
    position = jnp.where(named, position, -1.0)[:, None, :]
    k = iota((experts, GROUP, length), 1)

    def placed(wanted):
        hit = position == wanted.astype(F32)
        return hit.astype(F32).reshape(experts * GROUP, length).astype(BF16)

    main = placed(jnp.where(k < CAP, k, -2))
    tail_rows = rows_ref[:, BLOCKS * block :]
    copies = []
    for j in range(BLOCKS):
        at = slice(j * block, (j + 1) * block)
        tail = placed(jnp.where(k == CAP, j, jnp.where(k == CAP + 1, BLOCKS + j, -2)))
        both = jnp.concatenate([main, tail], axis=1)
        source = jnp.concatenate([rows_ref[:, at], tail_rows], axis=0)
        out_ref[:, at] = dot(both, source).astype(BF16)
        copies += start((out_ref.at[:, at], out_hbm.at[:, at], sems.at[j]))
    finish(copies)


def expert_kernel(
    x_ref, gate_a, up_a, down_a, gate_b, up_b, down_b, out_hbm,
    gate_ref, up_ref, down_ref, rows_ref, act_ref, out_ref, sems,
):
    chunk_rows, wide = x_ref.shape
    block = wide // BLOCKS
    half = gate_a.shape[1]
    low, high = slice(0, half), slice(half, 2 * half)
    first, second = slice(0, gate_a.shape[0] // 2), slice(gate_a.shape[0] // 2, gate_a.shape[0])
    parts = [
        start(
            (gate_a.at[k], gate_ref.at[k, low], sems.at[4 * i]),
            (gate_b.at[k], gate_ref.at[k, high], sems.at[4 * i + 1]),
            (up_a.at[k], up_ref.at[k, low], sems.at[4 * i + 2]),
            (up_b.at[k], up_ref.at[k, high], sems.at[4 * i + 3]),
        )
        for i, k in enumerate((first, second))
    ]
    downs = start((down_a, down_ref.at[low], sems.at[8]), (down_b, down_ref.at[high], sems.at[9]))

    step = 256
    chunks = step // GROUP
    packed = chunks * CAP

    def onehot(q, c, j=None):
        k, sub = q // chunks, c % GROUP
        if j is None:
            hit = sub == k
        else:
            hit = ((k == j) & (sub == CAP)) | ((k == BLOCKS + j) & (sub == CAP + 1))
        hit = hit & (c // GROUP == q % chunks)
        return hit.astype(F32).astype(BF16)

    q, c = iota((packed, step), 0), iota((packed, step), 1)
    main = onehot(q, c)
    tail = jnp.concatenate([onehot(q, c, j) for j in range(BLOCKS)], axis=1)
    groups = range(chunk_rows // step)
    for g in groups:
        source, target = slice(g * step, (g + 1) * step), slice(g * packed, (g + 1) * packed)
        rows_ref[target, :wide] = dot(main, x_ref[source, :]).astype(BF16)
        stacked = jnp.concatenate(
            [x_ref[source, j * block : (j + 1) * block] for j in range(BLOCKS)], axis=0
        )
        rows_ref[target, wide:] = dot(tail, stacked).astype(BF16)

    finish(parts[0])
    gate, up = dot(rows_ref[:, first], gate_ref[first]), dot(rows_ref[:, first], up_ref[first])
    finish(parts[1])
    gate = gate + dot(rows_ref[:, second], gate_ref[second])
    up = up + dot(rows_ref[:, second], up_ref[second])
    act_ref[...] = (gate / (1.0 + jnp.exp(-gate)) * up).astype(BF16)
    finish(downs)
    last = dot(act_ref[...], down_ref[:, wide:]).astype(BF16)
    q, c = iota((step, packed), 1), iota((step, packed), 0)
    main = onehot(q, c)
    copies = []
    for j in range(BLOCKS):
        at = slice(j * block, (j + 1) * block)
        spread = jnp.concatenate([main, onehot(q, c, j)], axis=1)
        result = dot(act_ref[...], down_ref[:, at]).astype(BF16)
        for g in groups:
            source, target = slice(g * packed, (g + 1) * packed), slice(g * step, (g + 1) * step)
            both = jnp.concatenate([result[source], last[source]], axis=0)
            out_ref[target, at] = dot(spread, both).astype(BF16)
        copies += start((out_ref.at[:, at], out_hbm.at[:, at], sems.at[10 + j]))
    finish(copies)


def combine_kernel(routes_ref, scale_ref, back_ref, out_hbm, out_ref, sems):
    length = routes_ref.shape[0]
    slots = back_ref.shape[0]
    experts = slots // GROUP
    block = back_ref.shape[1] // BLOCKS
    scale = scale_ref[...]
    share = scale / jnp.sum(scale, axis=1, keepdims=True)
    expert = iota((length, experts), 1)
    hits = [expert == routes_ref[:, r : r + 1] for r in range(2)]
    named = (hits[0] | hits[1]).astype(F32).astype(BF16)
    earlier = (iota((length, length), 1) < iota((length, length), 0)).astype(F32).astype(BF16)
    position = dot(earlier, named)
    slot = iota((length, slots), 1)
    places = []
    for r in range(2):
        k = jnp.sum(jnp.where(hits[r], position, 0.0), axis=1, keepdims=True).astype(I32)
        places.append((k, routes_ref[:, r : r + 1] * GROUP))

    def onehot(index):
        return (slot == index).astype(F32).astype(BF16)

    main = [onehot(base + k) for k, base in places]
    tails = [jnp.zeros((length, block), F32) for _ in range(2)]
    copies = []
    for j in range(BLOCKS):
        at = slice(j * block, (j + 1) * block)
        picks = list(main)
        for k, base in places:
            second = k >= BLOCKS
            mine = jnp.where(second, k - BLOCKS, k) == j
            picks.append(onehot(jnp.where(mine, base + CAP + second.astype(I32), -1)))
        got = dot(jnp.concatenate(picks, axis=0), back_ref[:, at])
        total = share[:, 0:1] * got[:length] + share[:, 1:2] * got[length : 2 * length]
        out_ref[:, at] = total.astype(BF16)
        copies += start((out_ref.at[:, at], out_hbm.at[:, at], sems.at[j]))
        for r in range(2):
            tails[r] = tails[r] + got[(2 + r) * length : (3 + r) * length]
    total = share[:, 0:1] * tails[0] + share[:, 1:2] * tails[1]
    at = slice(BLOCKS * block, (BLOCKS + 1) * block)
    out_ref[:, at] = total.astype(BF16)
    finish(copies + start((out_ref.at[:, at], out_hbm.at[:, at], sems.at[BLOCKS])))


def call(kernel, out, *args, flops, scratch, sems, here=(), limit=32 << 20):
    moved = sum(a.size * a.dtype.itemsize for a in args) + out[0] * out[1] * 2
    return pl.pallas_call(
        kernel,
        out_shape=jax.ShapeDtypeStruct(out, BF16),
        in_specs=[VMEM if i in here else ANY for i in range(len(args))],
        out_specs=ANY,
        scratch_shapes=[pltpu.VMEM(*s) for s in scratch] + [pltpu.SemaphoreType.DMA((sems,))],
        compiler_params=pltpu.CompilerParams(vmem_limit_bytes=limit),
        cost_estimate=pl.CostEstimate(flops=flops, bytes_accessed=moved, transcendentals=0),
    )(*args)


def pack(counts, owner, rows, length):
    width = rows.shape[1]
    return call(
        pack_kernel, (length, width), counts, owner, rows,
        flops=2 * length * rows.shape[0] * width,
        scratch=[
            (counts.shape, I32), (owner.shape, I32), (rows.shape, BF16), ((length, width), BF16),
        ],
        sems=4, limit=62 << 20,
    )


def dispatch(routes_t, sequence, slots, wide):
    length = sequence.shape[0]
    return call(
        dispatch_kernel, (slots, wide), routes_t, sequence,
        flops=4 * slots * length * wide,
        scratch=[((slots, wide), BF16)], sems=BLOCKS, here=(0, 1),
    )


def run_expert(received, own, other):
    slots, wide = received.shape
    width, half = own[0].shape
    rows = slots // GROUP * CAP
    return call(
        expert_kernel, (slots, wide), received, *own, *other,
        flops=12 * slots * width * half,
        scratch=[
            ((width, 2 * half), BF16), ((width, 2 * half), BF16), ((2 * half, width), BF16),
            ((rows, width), BF16), ((rows, 2 * half), BF16), ((slots, wide), BF16),
        ],
        sems=10 + BLOCKS, here=(0,), limit=48 << 20,
    )


def combine(routes, route_scale, returned, width):
    length, slots = routes.shape[0], returned.shape[0]
    return call(
        combine_kernel, (length, width), routes, route_scale, returned,
        flops=8 * length * slots * returned.shape[1],
        scratch=[((length, width), BF16)], sems=BLOCKS + 1, here=(0, 1, 2),
    )


def local(image_rows, image_counts, image_owner, routes, route_scale, w_gate, w_up, w_down):
    owners = lax.axis_size(("dp", "mp"))
    experts = lax.axis_size("expert")
    length = routes.shape[0]
    width = image_rows.shape[1]
    slots = experts * GROUP
    wide = width // (BLOCKS + 1) * BLOCKS
    own = [w_gate[0], w_up[0], w_down[0]]
    other = [lax.ppermute(w, "mp", [(0, 1), (1, 0)]) for w in own]

    outgoing = pack(image_counts, image_owner, image_rows, length)
    arrived = lax.all_to_all(
        outgoing.reshape(owners, length // owners, width),
        ("dp", "mp"),
        split_axis=0,
        concat_axis=0,
        tiled=True,
    )
    buffer = dispatch(routes.T, arrived.reshape(length, width), slots, wide)

    def exchange(x):
        y = lax.all_to_all(
            x.reshape(experts, GROUP, wide), "expert", split_axis=0, concat_axis=0, tiled=True
        )
        return y.reshape(slots, wide)

    returned = exchange(run_expert(exchange(buffer), own, other))
    return combine(routes, route_scale, returned, width)


def solution(mesh):
    return jax.shard_map(
        local,
        mesh=mesh,
        in_specs=(
            P(("dp", "expert", "mp"), None),
            P(("dp", "expert", "mp"), None),
            P(("dp", "expert", "mp"), None),
            P(("dp", "expert", "mp"), None),
            P(("dp", "expert", "mp"), None),
            P("expert", None, "mp"),
            P("expert", None, "mp"),
            P("expert", "mp", None),
        ),
        out_specs=P(("dp", "expert", "mp"), None),
        check_vma=False,
    )
```

time: 162 us -> 153 us (0.944)
  local copies, waits for them, and re-layouts: 13 us -> 1.4 us
  waiting for transfers between devices: 72.3 us -> 74.5 us
    unnamed x30 -> x12, local copies, waits for them, and re-layouts: 13 us -> 1.4 us
  transfers between devices with their start and end apart: 5 -> 5, of which waited for: 3 -> 4; matrix products, arithmetic and copies ran while one was open for 0% -> 0% of each run, Pallas kernels for 0% -> 0%
where the time goes in v2:
time: 153 us
  waiting for transfers between devices  74.5 us (49%)
  starting transfers between devices  39.5 us (26%)
  blocking collectives  22.9 us (15%)
  Pallas kernels  14.5 us (9%)
    all_to_all x2, waiting for transfers between devices, exchange(): lax.all_to_all(x.reshape(experts, GROUP, wide), 'expert', split_axis=0, c...  72.2 us
    all_to_all x2, starting transfers between devices, exchange(): lax.all_to_all(x.reshape(experts, GROUP, wide), 'expert', split_axis=0, c...  32.1 us
    all_to_all x1, blocking collectives, local(): lax.all_to_all(outgoing.reshape(owners, length // owners, width), ('dp',...  22.9 us
    pallas_call x4, Pallas kernels, call(): pl.pallas_call(kernel, out_shape=jax.ShapeDtypeStruct(out, BF16), in_spec...  14.5 us
    ppermute x3, starting transfers between devices, local(): other = [lax.ppermute(w, 'mp', [(0, 1), (1, 0)]) for w in own]  7.38 us
  transfers between devices with their start and end apart: 5, of which 4 were waited for; matrix products, arithmetic and copies ran while one was open for 0% of the time, Pallas kernels for 0%

profile of v2, /device:TPU:16, one launch (start us, length us, event | category | flops | bytes accessed | tf_op | source)
XLA Modules:
  0.0 152.9 jit_solution(16313345737992765148)
XLA Ops:
  0.0 0.0 copy-start
  0.0 2.1 %shard_map.82 = bf16[128,2048]{1,0:T(8,128)(2,1)} custom-call(s32[1,16]{1,0:T(1,128)} %counts_hbm.1, s32[1,16]{1,0:T(1,128)} %owner_hbm.1, bf16[80,2048]{1,0:T(8,128)(2,1)} %rows_hbm.1), custom_call_target="tpu_custom_call" | custom-call | flops 41943040 | bytes 852096 | tf_op jit(solution)/shard_map/pallas_call | solution.py:206
  2.1 22.9 %all_to_all.15 = bf16[16,8,2048]{2,1,0:T(8,128)(2,1)S(1)} all-to-all(bf16[16,8,2048]{2,1,0:T(8,128)(2,1)} %bitcast.16), channel_id=1, replica_groups=mesh['dp'=8,'expert'=64,'mp'=2] {'dp','mp'}, dimensions={0} | all-to-all | bytes 1048576 | tf_op jit(solution)/shard_map/all_to_all | solution.py:273
  25.0 0.0 copy-done
  25.0 1.6 %shard_map.83 = bf16[512,1536]{1,0:T(8,128)(2,1)} custom-call(s32[2,128]{1,0:T(2,128)S(1)} %bitcast.13, bf16[128,2048]{1,0:T(8,128)(2,1)S(1)} %bitcast.10), custom_call_target="tpu_custom_call" | custom-call | flops 402653184 | bytes 2098176 | tf_op jit(solution)/shard_map/pallas_call | solution.py:206
  26.7 0.0 copy-start.1
  26.7 23.4 %all-to-all-start.1 = ((bf16[64,8,1536]{2,1,0:T(8,128)(2,1)}), bf16[64,8,1536]{2,1,0:T(8,128)(2,1)S(1)}, u32[]{:S(2)}, u32[]{:S(2)}) async-start(bf16[64,8,1536]{2,1,0:T(8,128)(2,1)} %bitcast.3), calls=%async_computation.1 | async-start | bytes 3145728 | tf_op jit(solution)/shard_map/all_to_all | solution.py:283
  50.2 0.0 copy-done.1
  50.2 3.0 %collective-permute-start = (bf16[2048,384]{1,0:T(8,128)(2,1)S(1)}, bf16[2048,384]{1,0:T(8,128)(2,1)S(1)}, u32[]{:S(2)}, u32[]{:S(2)}) collective-permute-start(bf16[2048,384]{1,0:T(8,128)(2,1)S(1)} %bitcast.14), channel_id=1, source_target_pairs={{0,1},{1,0},{2,3},{3,2},{4,5},{5,4},{6,7},{7,6},{8,9},{9,8},{10,11... | collective-permute-start | bytes 4718600 | tf_op jit(solution)/shard_map/ppermute | solution.py:270
  53.2 1.9 %collective-permute-start.1 = (bf16[2048,384]{1,0:T(8,128)(2,1)}, bf16[2048,384]{1,0:T(8,128)(2,1)S(1)}, u32[]{:S(2)}, u32[]{:S(2)}) collective-permute-start(bf16[2048,384]{1,0:T(8,128)(2,1)} %bitcast.17), channel_id=1, source_target_pairs={{0,1},{1,0},{2,3},{3,2},{4,5},{5,4},{6,7},{7,6},{8,9},{9,8},{10,11... | collective-permute-start | bytes 4718600 | tf_op jit(solution)/shard_map/ppermute | solution.py:270
  55.1 2.4 %collective-permute-start.2 = (bf16[384,2048]{1,0:T(8,128)(2,1)}, bf16[384,2048]{1,0:T(8,128)(2,1)}, u32[]{:S(2)}, u32[]{:S(2)}) collective-permute-start(bf16[384,2048]{1,0:T(8,128)(2,1)} %bitcast.19), channel_id=1, source_target_pairs={{0,1},{1,0},{2,3},{3,2},{4,5},{5,4},{6,7},{7,6},{8,9},{9,8},{10,11... | collective-permute-start | bytes 4718600 | tf_op jit(solution)/shard_map/ppermute | solution.py:270
  57.6 0.0 collective-permute-done.gate_b
  57.6 0.0 copy-start.3
  57.6 1.1 collective-permute-done.1.up_b
  58.7 0.0 copy-done.3
  58.7 0.0 copy-start.4
  58.7 1.2 copy-done.4
  59.9 1.2 collective-permute-done.2.down_b
  61.1 30.6 %all-to-all-done.1 = bf16[64,8,1536]{2,1,0:T(8,128)(2,1)S(1)} async-done(((bf16[64,8,1536]{2,1,0:T(8,128)(2,1)}), bf16[64,8,1536]{2,1,0:T(8,128)(2,1)S(1)}, u32[]{:S(2)}, u32[]{:S(2)}) %all-to-all-start.1) | async-done | bytes 1572896 | tf_op jit(solution)/shard_map/all_to_all | solution.py:283
  91.7 8.6 %shard_map.84 = bf16[512,1536]{1,0:T(8,128)(2,1)} custom-call(bf16[512,1536]{1,0:T(8,128)(2,1)S(1)} %bitcast.11, bf16[2048,384]{1,0:T(8,128)(2,1)S(1)} %bitcast.15, bf16[2048,384]{1,0:T(8,128)(2,1)} %bitcast.18, bf16[384,2048]{1,0:T(8,128)(2,1)} %bitcast.20, bf16[2048,384]{1,0:T(8,128)(2,1)} %copy-done.3, bf16[2048,384]{1,0:T(8,128)(2,1)} %copy-done.4, ...), custom_call_target="tpu_custom_call" | custom-call | flops 4831838208 | bytes 12582912 | tf_op jit(solution)/shard_map/pallas_call | solution.py:206
  100.3 0.0 copy-start.2
  100.3 8.7 %all-to-all-start.2 = ((bf16[64,8,1536]{2,1,0:T(8,128)(2,1)}), bf16[64,8,1536]{2,1,0:T(8,128)(2,1)S(1)}, u32[]{:S(2)}, u32[]{:S(2)}) async-start(bf16[64,8,1536]{2,1,0:T(8,128)(2,1)} %bitcast.8), calls=%async_computation.2 | async-start | bytes 3145728 | tf_op jit(solution)/shard_map/all_to_all | solution.py:283
  109.0 0.1 copy.9.routes_ref
  109.1 0.0 copy-done.2
  109.1 0.1 copy.10.scale_ref
  109.2 41.5 %all-to-all-done.2 = bf16[64,8,1536]{2,1,0:T(8,128)(2,1)S(1)} async-done(((bf16[64,8,1536]{2,1,0:T(8,128)(2,1)}), bf16[64,8,1536]{2,1,0:T(8,128)(2,1)S(1)}, u32[]{:S(2)}, u32[]{:S(2)}) %all-to-all-start.2) | async-done | bytes 1572896 | tf_op jit(solution)/shard_map/all_to_all | solution.py:283
  150.8 2.2 %shard_map.85 = bf16[128,2048]{1,0:T(8,128)(2,1)} custom-call(s32[128,2]{1,0:T(8,128)S(1)} %copy.9.routes_ref, f32[128,2]{1,0:T(8,128)S(1)} %copy.10.scale_ref, bf16[512,1536]{1,0:T(8,128)(2,1)S(1)} %bitcast.12), custom_call_target="tpu_custom_call" | custom-call | flops 805306368 | bytes 2099200 | tf_op jit(solution)/shard_map/pallas_call | solution.py:206
Async XLA Ops:
  0.0 25.0 %copy-start = (s32[128,2]{0,1:T(2,128)S(1)}, s32[128,2]{0,1:T(2,128)}, u32[]{:S(2)}) copy-start(s32[128,2]{0,1:T(2,128)} %param.11) | copy-start | bytes 3076
  26.7 23.5 %copy-start.1 = (bf16[1,2048,384]{2,1,0:T(8,128)(2,1)S(1)}, bf16[1,2048,384]{2,1,0:T(8,128)(2,1)}, u32[]{:S(2)}) copy-start(bf16[1,2048,384]{2,1,0:T(8,128)(2,1)} %param.13) | copy-start | bytes 4718596
  26.7 65.0 %all-to-all-start.1 = ((bf16[64,8,1536]{2,1,0:T(8,128)(2,1)}), bf16[64,8,1536]{2,1,0:T(8,128)(2,1)S(1)}, u32[]{:S(2)}, u32[]{:S(2)}) async-start(bf16[64,8,1536]{2,1,0:T(8,128)(2,1)} %bitcast.3), calls=%async_computation.1 | async-start | bytes 3145728 | tf_op jit(solution)/shard_map/all_to_all | solution.py:283
  50.2 7.4 %collective-permute-start = (bf16[2048,384]{1,0:T(8,128)(2,1)S(1)}, bf16[2048,384]{1,0:T(8,128)(2,1)S(1)}, u32[]{:S(2)}, u32[]{:S(2)}) collective-permute-start(bf16[2048,384]{1,0:T(8,128)(2,1)S(1)} %bitcast.14), channel_id=1, source_target_pairs={{0,1},{1,0},{2,3},{3,2},{4,5},{5,4},{6,7},{7,6},{8,9},{9,8},{10,11... | collective-permute-start | bytes 4718600 | tf_op jit(solution)/shard_map/ppermute | solution.py:270
  53.2 5.5 %collective-permute-start.1 = (bf16[2048,384]{1,0:T(8,128)(2,1)}, bf16[2048,384]{1,0:T(8,128)(2,1)S(1)}, u32[]{:S(2)}, u32[]{:S(2)}) collective-permute-start(bf16[2048,384]{1,0:T(8,128)(2,1)} %bitcast.17), channel_id=1, source_target_pairs={{0,1},{1,0},{2,3},{3,2},{4,5},{5,4},{6,7},{7,6},{8,9},{9,8},{10,11... | collective-permute-start | bytes 4718600 | tf_op jit(solution)/shard_map/ppermute | solution.py:270
  55.1 6.0 %collective-permute-start.2 = (bf16[384,2048]{1,0:T(8,128)(2,1)}, bf16[384,2048]{1,0:T(8,128)(2,1)}, u32[]{:S(2)}, u32[]{:S(2)}) collective-permute-start(bf16[384,2048]{1,0:T(8,128)(2,1)} %bitcast.19), channel_id=1, source_target_pairs={{0,1},{1,0},{2,3},{3,2},{4,5},{5,4},{6,7},{7,6},{8,9},{9,8},{10,11... | collective-permute-start | bytes 4718600 | tf_op jit(solution)/shard_map/ppermute | solution.py:270
  57.6 1.2 copy-start.3
  58.7 1.2 copy-start.4
  100.3 8.8 %copy-start.2 = (f32[128,2]{0,1:T(2,128)S(1)}, f32[128,2]{0,1:T(2,128)}, u32[]{:S(2)}) copy-start(f32[128,2]{0,1:T(2,128)} %param.12) | copy-start | bytes 3076
  100.3 50.4 %all-to-all-start.2 = ((bf16[64,8,1536]{2,1,0:T(8,128)(2,1)}), bf16[64,8,1536]{2,1,0:T(8,128)(2,1)S(1)}, u32[]{:S(2)}, u32[]{:S(2)}) async-start(bf16[64,8,1536]{2,1,0:T(8,128)(2,1)} %bitcast.8), calls=%async_computation.2 | async-start | bytes 3145728 | tf_op jit(solution)/shard_map/all_to_all | solution.py:283

commit v3 on v2

--- a/solution.py
+++ b/solution.py
@@ -98,7 +98,9 @@
     block = wide // BLOCKS
     half = gate_a.shape[1]
     low, high = slice(0, half), slice(half, 2 * half)
-    first, second = slice(0, gate_a.shape[0] // 2), slice(gate_a.shape[0] // 2, gate_a.shape[0])
+    cuts = 4
+    deep = gate_a.shape[0] // cuts
+    steps = [slice(i * deep, (i + 1) * deep) for i in range(cuts)]
     parts = [
         start(
             (gate_a.at[k], gate_ref.at[k, low], sems.at[4 * i]),
@@ -106,86 +108,86 @@
             (up_a.at[k], up_ref.at[k, low], sems.at[4 * i + 2]),
             (up_b.at[k], up_ref.at[k, high], sems.at[4 * i + 3]),
         )
-        for i, k in enumerate((first, second))
+        for i, k in enumerate(steps)
     ]
-    downs = start((down_a, down_ref.at[low], sems.at[8]), (down_b, down_ref.at[high], sems.at[9]))
+    downs = start(
+        (down_a, down_ref.at[low], sems.at[4 * cuts]),
+        (down_b, down_ref.at[high], sems.at[4 * cuts + 1]),
+    )
 
     step = 256
     chunks = step // GROUP
     packed = chunks * CAP
 
-    def onehot(q, c, j=None):
-        k, sub = q // chunks, c % GROUP
-        if j is None:
-            hit = sub == k
-        else:
-            hit = ((k == j) & (sub == CAP)) | ((k == BLOCKS + j) & (sub == CAP + 1))
-        hit = hit & (c // GROUP == q % chunks)
-        return hit.astype(F32).astype(BF16)
-
-    q, c = iota((packed, step), 0), iota((packed, step), 1)
-    main = onehot(q, c)
-    tail = jnp.concatenate([onehot(q, c, j) for j in range(BLOCKS)], axis=1)
+    def onehot(t, c):
+        return ((c // GROUP == t % chunks) & (c % GROUP == t // chunks)).astype(F32).astype(BF16)
+
+    gather = onehot(iota((step, step), 0), iota((step, step), 1))
+    spread = onehot(iota((step, step), 1), iota((step, step), 0))
     groups = range(chunk_rows // step)
     for g in groups:
-        source, target = slice(g * step, (g + 1) * step), slice(g * packed, (g + 1) * packed)
-        rows_ref[target, :wide] = dot(main, x_ref[source, :]).astype(BF16)
-        stacked = jnp.concatenate(
-            [x_ref[source, j * block : (j + 1) * block] for j in range(BLOCKS)], axis=0
-        )
-        rows_ref[target, wide:] = dot(tail, stacked).astype(BF16)
-
-    finish(parts[0])
-    gate, up = dot(rows_ref[:, first], gate_ref[first]), dot(rows_ref[:, first], up_ref[first])
-    finish(parts[1])
-    gate = gate + dot(rows_ref[:, second], gate_ref[second])
-    up = up + dot(rows_ref[:, second], up_ref[second])
+        for j in range(BLOCKS):
+            at = slice(j * block, (j + 1) * block)
+            moved = dot(gather, x_ref[g * step : (g + 1) * step, at]).astype(BF16)
+            rows_ref[g * packed : (g + 1) * packed, at] = moved[:packed]
+            for i, k in enumerate((j, BLOCKS + j)):
+                target = g * packed + k * chunks
+                rows_ref[target : target + chunks, wide:] = moved[packed + i * chunks :][:chunks]
+
+    gate = up = 0.0
+    for k, copies in zip(steps, parts):
+        finish(copies)
+        gate = gate + dot(rows_ref[:, k], gate_ref[k])
+        up = up + dot(rows_ref[:, k], up_ref[k])
     act_ref[...] = (gate / (1.0 + jnp.exp(-gate)) * up).astype(BF16)
     finish(downs)
     last = dot(act_ref[...], down_ref[:, wide:]).astype(BF16)
-    q, c = iota((step, packed), 1), iota((step, packed), 0)
-    main = onehot(q, c)
     copies = []
     for j in range(BLOCKS):
         at = slice(j * block, (j + 1) * block)
-        spread = jnp.concatenate([main, onehot(q, c, j)], axis=1)
         result = dot(act_ref[...], down_ref[:, at]).astype(BF16)
         for g in groups:
-            source, target = slice(g * packed, (g + 1) * packed), slice(g * step, (g + 1) * step)
-            both = jnp.concatenate([result[source], last[source]], axis=0)
-            out_ref[target, at] = dot(spread, both).astype(BF16)
-        copies += start((out_ref.at[:, at], out_hbm.at[:, at], sems.at[10 + j]))
+            source, target = g * packed, slice(g * step, (g + 1) * step)
+            tails = [source + (j + k) * chunks for k in (0, BLOCKS)]
+            both = [result[source : source + packed]] + [last[i : i + chunks] for i in tails]
+            out_ref[target, at] = dot(spread, jnp.concatenate(both, axis=0)).astype(BF16)
+        copies += start((out_ref.at[:, at], out_hbm.at[:, at], sems.at[4 * cuts + 2 + j]))
     finish(copies)
 
 
-def combine_kernel(routes_ref, scale_ref, back_ref, out_hbm, out_ref, sems):
+def places_kernel(routes_ref, scale_ref, at_ref, share_ref):
     length = routes_ref.shape[0]
-    slots = back_ref.shape[0]
-    experts = slots // GROUP
-    block = back_ref.shape[1] // BLOCKS
     scale = scale_ref[...]
-    share = scale / jnp.sum(scale, axis=1, keepdims=True)
-    expert = iota((length, experts), 1)
+    share_ref[...] = scale / jnp.sum(scale, axis=1, keepdims=True)
+    expert = iota((length, 128), 1)
     hits = [expert == routes_ref[:, r : r + 1] for r in range(2)]
     named = (hits[0] | hits[1]).astype(F32).astype(BF16)
     earlier = (iota((length, length), 1) < iota((length, length), 0)).astype(F32).astype(BF16)
     position = dot(earlier, named)
-    slot = iota((length, slots), 1)
-    places = []
     for r in range(2):
         k = jnp.sum(jnp.where(hits[r], position, 0.0), axis=1, keepdims=True).astype(I32)
-        places.append((k, routes_ref[:, r : r + 1] * GROUP))
+        at_ref[:, r : r + 1] = routes_ref[:, r : r + 1] * GROUP + k
+
+
+def combine_kernel(at_ref, share_ref, back_ref, out_hbm, out_ref, sems):
+    length = at_ref.shape[0]
+    slots = back_ref.shape[0]
+    block = back_ref.shape[1] // BLOCKS
+    share = share_ref[...]
+    slot = iota((length, slots), 1)
+    places = [at_ref[:, r : r + 1] for r in range(2)]
 
     def onehot(index):
         return (slot == index).astype(F32).astype(BF16)
 
-    main = [onehot(base + k) for k, base in places]
+    main = [onehot(place) for place in places]
     tails = [jnp.zeros((length, block), F32) for _ in range(2)]
     copies = []
     for j in range(BLOCKS):
         at = slice(j * block, (j + 1) * block)
         picks = list(main)
-        for k, base in places:
+        for place in places:
+            k, base = place % GROUP, place - place % GROUP
             second = k >= BLOCKS
             mine = jnp.where(second, k - BLOCKS, k) == j
             picks.append(onehot(jnp.where(mine, base + CAP + second.astype(I32), -1)))
@@ -246,14 +248,22 @@
             ((width, 2 * half), BF16), ((width, 2 * half), BF16), ((2 * half, width), BF16),
             ((rows, width), BF16), ((rows, 2 * half), BF16), ((slots, wide), BF16),
         ],
-        sems=10 + BLOCKS, here=(0,), limit=48 << 20,
+        sems=18 + BLOCKS, here=(0,), limit=48 << 20,
     )
 
 
 def combine(routes, route_scale, returned, width):
     length, slots = routes.shape[0], returned.shape[0]
+    at, share = pl.pallas_call(
+        places_kernel,
+        out_shape=[
+            jax.ShapeDtypeStruct(routes.shape, I32),
+            jax.ShapeDtypeStruct(routes.shape, F32),
+        ],
+        compiler_params=pltpu.CompilerParams(vmem_limit_bytes=16 << 20),
+    )(routes, route_scale)
     return call(
-        combine_kernel, (length, width), routes, route_scale, returned,
+        combine_kernel, (length, width), at, share, returned,
         flops=8 * length * slots * returned.shape[1],
         scratch=[((length, width), BF16)], sems=BLOCKS + 1, here=(0, 1, 2),
     )

time: 153 us -> 152 us (level)
  no operation moved by 1% of the time
where the time goes in v3:
time: 152 us
  waiting for transfers between devices  74.2 us (49%)
  starting transfers between devices  39.5 us (26%)
  blocking collectives  22.9 us (15%)
  Pallas kernels  13.6 us (9%)
    all_to_all x2, waiting for transfers between devices, exchange(): lax.all_to_all(x.reshape(experts, GROUP, wide), 'expert', split_axis=0, c...  71.8 us
    all_to_all x2, starting transfers between devices, exchange(): lax.all_to_all(x.reshape(experts, GROUP, wide), 'expert', split_axis=0, c...  32.1 us
    all_to_all x1, blocking collectives, local(): lax.all_to_all(outgoing.reshape(owners, length // owners, width), ('dp',...  22.9 us
    pallas_call x4, Pallas kernels, call(): pl.pallas_call(kernel, out_shape=jax.ShapeDtypeStruct(out, BF16), in_spec...  13.3 us
    ppermute x3, starting transfers between devices, local(): other = [lax.ppermute(w, 'mp', [(0, 1), (1, 0)]) for w in own]  7.38 us
  transfers between devices with their start and end apart: 5, of which 4 were waited for; matrix products, arithmetic and copies ran while one was open for 0% of the time, Pallas kernels for 0%

profile of v3, /device:TPU:16, one launch (start us, length us, event | category | flops | bytes accessed | tf_op | source)
XLA Modules:
  0.0 151.7 jit_solution(7237232947378074881)
XLA Ops:
  0.0 0.0 copy-start
  0.0 2.1 %shard_map.83 = bf16[128,2048]{1,0:T(8,128)(2,1)} custom-call(s32[1,16]{1,0:T(1,128)} %counts_hbm.1, s32[1,16]{1,0:T(1,128)} %owner_hbm.1, bf16[80,2048]{1,0:T(8,128)(2,1)} %rows_hbm.1), custom_call_target="tpu_custom_call" | custom-call | flops 41943040 | bytes 852096 | tf_op jit(solution)/shard_map/pallas_call | solution.py:208
  2.1 22.9 %all_to_all.15 = bf16[16,8,2048]{2,1,0:T(8,128)(2,1)S(1)} all-to-all(bf16[16,8,2048]{2,1,0:T(8,128)(2,1)} %bitcast.16), channel_id=1, replica_groups=mesh['dp'=8,'expert'=64,'mp'=2] {'dp','mp'}, dimensions={0} | all-to-all | bytes 1048576 | tf_op jit(solution)/shard_map/all_to_all | solution.py:283
  25.0 0.0 copy-done
  25.0 1.7 %shard_map.84 = bf16[512,1536]{1,0:T(8,128)(2,1)} custom-call(s32[2,128]{1,0:T(2,128)S(1)} %bitcast.13, bf16[128,2048]{1,0:T(8,128)(2,1)S(1)} %bitcast.10), custom_call_target="tpu_custom_call" | custom-call | flops 402653184 | bytes 2098176 | tf_op jit(solution)/shard_map/pallas_call | solution.py:208
  26.7 0.0 copy-start.1
  26.7 23.4 %all-to-all-start.1 = ((bf16[64,8,1536]{2,1,0:T(8,128)(2,1)}), bf16[64,8,1536]{2,1,0:T(8,128)(2,1)S(1)}, u32[]{:S(2)}, u32[]{:S(2)}) async-start(bf16[64,8,1536]{2,1,0:T(8,128)(2,1)} %bitcast.3), calls=%async_computation.1 | async-start | bytes 3145728 | tf_op jit(solution)/shard_map/all_to_all | solution.py:293
  50.2 0.0 copy-done.1
  50.2 3.0 %collective-permute-start = (bf16[2048,384]{1,0:T(8,128)(2,1)S(1)}, bf16[2048,384]{1,0:T(8,128)(2,1)S(1)}, u32[]{:S(2)}, u32[]{:S(2)}) collective-permute-start(bf16[2048,384]{1,0:T(8,128)(2,1)S(1)} %bitcast.14), channel_id=1, source_target_pairs={{0,1},{1,0},{2,3},{3,2},{4,5},{5,4},{6,7},{7,6},{8,9},{9,8},{10,11... | collective-permute-start | bytes 4718600 | tf_op jit(solution)/shard_map/ppermute | solution.py:280
  53.2 1.9 %collective-permute-start.1 = (bf16[2048,384]{1,0:T(8,128)(2,1)}, bf16[2048,384]{1,0:T(8,128)(2,1)S(1)}, u32[]{:S(2)}, u32[]{:S(2)}) collective-permute-start(bf16[2048,384]{1,0:T(8,128)(2,1)} %bitcast.17), channel_id=1, source_target_pairs={{0,1},{1,0},{2,3},{3,2},{4,5},{5,4},{6,7},{7,6},{8,9},{9,8},{10,11... | collective-permute-start | bytes 4718600 | tf_op jit(solution)/shard_map/ppermute | solution.py:280
  55.2 2.4 %collective-permute-start.2 = (bf16[384,2048]{1,0:T(8,128)(2,1)}, bf16[384,2048]{1,0:T(8,128)(2,1)}, u32[]{:S(2)}, u32[]{:S(2)}) collective-permute-start(bf16[384,2048]{1,0:T(8,128)(2,1)} %bitcast.19), channel_id=1, source_target_pairs={{0,1},{1,0},{2,3},{3,2},{4,5},{5,4},{6,7},{7,6},{8,9},{9,8},{10,11... | collective-permute-start | bytes 4718600 | tf_op jit(solution)/shard_map/ppermute | solution.py:280
  57.6 0.0 collective-permute-done.gate_b
  57.6 0.0 copy-start.3
  57.6 1.1 collective-permute-done.1.up_b
  58.8 0.0 copy-done.3
  58.8 0.0 copy-start.4
  58.8 1.1 copy-done.4
  59.9 1.2 collective-permute-done.2.down_b
  61.1 30.6 %all-to-all-done.1 = bf16[64,8,1536]{2,1,0:T(8,128)(2,1)S(1)} async-done(((bf16[64,8,1536]{2,1,0:T(8,128)(2,1)}), bf16[64,8,1536]{2,1,0:T(8,128)(2,1)S(1)}, u32[]{:S(2)}, u32[]{:S(2)}) %all-to-all-start.1) | async-done | bytes 1572896 | tf_op jit(solution)/shard_map/all_to_all | solution.py:293
  91.8 7.7 %shard_map.85 = bf16[512,1536]{1,0:T(8,128)(2,1)} custom-call(bf16[512,1536]{1,0:T(8,128)(2,1)S(1)} %bitcast.11, bf16[2048,384]{1,0:T(8,128)(2,1)S(1)} %bitcast.15, bf16[2048,384]{1,0:T(8,128)(2,1)} %bitcast.18, bf16[384,2048]{1,0:T(8,128)(2,1)} %bitcast.20, bf16[2048,384]{1,0:T(8,128)(2,1)} %copy-done.3, bf16[2048,384]{1,0:T(8,128)(2,1)} %copy-done.4, ...), custom_call_target="tpu_custom_call" | custom-call | flops 4831838208 | bytes 12582912 | tf_op jit(solution)/shard_map/pallas_call | solution.py:208
  99.5 0.0 copy-start.2
  99.5 8.7 %all-to-all-start.2 = ((bf16[64,8,1536]{2,1,0:T(8,128)(2,1)}), bf16[64,8,1536]{2,1,0:T(8,128)(2,1)S(1)}, u32[]{:S(2)}, u32[]{:S(2)}) async-start(bf16[64,8,1536]{2,1,0:T(8,128)(2,1)} %bitcast.8), calls=%async_computation.2 | async-start | bytes 3145728 | tf_op jit(solution)/shard_map/all_to_all | solution.py:293
  108.2 0.1 copy.9.routes_ref
  108.3 0.0 copy-done.2
  108.3 0.1 copy.10.scale_ref
  108.4 0.3 shard_map.82
  108.8 41.2 %all-to-all-done.2 = bf16[64,8,1536]{2,1,0:T(8,128)(2,1)S(1)} async-done(((bf16[64,8,1536]{2,1,0:T(8,128)(2,1)}), bf16[64,8,1536]{2,1,0:T(8,128)(2,1)S(1)}, u32[]{:S(2)}, u32[]{:S(2)}) %all-to-all-start.2) | async-done | bytes 1572896 | tf_op jit(solution)/shard_map/all_to_all | solution.py:293
  150.0 1.7 %shard_map.86 = bf16[128,2048]{1,0:T(8,128)(2,1)} custom-call(s32[128,2]{1,0:T(8,128)S(1)} %get-tuple-element.7.at_ref, f32[128,2]{1,0:T(8,128)S(1)} %get-tuple-element.8.share_ref, bf16[512,1536]{1,0:T(8,128)(2,1)S(1)} %bitcast.12), custom_call_target="tpu_custom_call" | custom-call | flops 805306368 | bytes 2099200 | tf_op jit(solution)/shard_map/pallas_call | solution.py:208
Async XLA Ops:
  0.0 25.0 %copy-start = (s32[128,2]{0,1:T(2,128)S(1)}, s32[128,2]{0,1:T(2,128)}, u32[]{:S(2)}) copy-start(s32[128,2]{0,1:T(2,128)} %param.11) | copy-start | bytes 3076
  26.7 23.5 %copy-start.1 = (bf16[1,2048,384]{2,1,0:T(8,128)(2,1)S(1)}, bf16[1,2048,384]{2,1,0:T(8,128)(2,1)}, u32[]{:S(2)}) copy-start(bf16[1,2048,384]{2,1,0:T(8,128)(2,1)} %param.13) | copy-start | bytes 4718596
  26.7 65.0 %all-to-all-start.1 = ((bf16[64,8,1536]{2,1,0:T(8,128)(2,1)}), bf16[64,8,1536]{2,1,0:T(8,128)(2,1)S(1)}, u32[]{:S(2)}, u32[]{:S(2)}) async-start(bf16[64,8,1536]{2,1,0:T(8,128)(2,1)} %bitcast.3), calls=%async_computation.1 | async-start | bytes 3145728 | tf_op jit(solution)/shard_map/all_to_all | solution.py:293
  50.2 7.4 %collective-permute-start = (bf16[2048,384]{1,0:T(8,128)(2,1)S(1)}, bf16[2048,384]{1,0:T(8,128)(2,1)S(1)}, u32[]{:S(2)}, u32[]{:S(2)}) collective-permute-start(bf16[2048,384]{1,0:T(8,128)(2,1)S(1)} %bitcast.14), channel_id=1, source_target_pairs={{0,1},{1,0},{2,3},{3,2},{4,5},{5,4},{6,7},{7,6},{8,9},{9,8},{10,11... | collective-permute-start | bytes 4718600 | tf_op jit(solution)/shard_map/ppermute | solution.py:280
  53.2 5.5 %collective-permute-start.1 = (bf16[2048,384]{1,0:T(8,128)(2,1)}, bf16[2048,384]{1,0:T(8,128)(2,1)S(1)}, u32[]{:S(2)}, u32[]{:S(2)}) collective-permute-start(bf16[2048,384]{1,0:T(8,128)(2,1)} %bitcast.17), channel_id=1, source_target_pairs={{0,1},{1,0},{2,3},{3,2},{4,5},{5,4},{6,7},{7,6},{8,9},{9,8},{10,11... | collective-permute-start | bytes 4718600 | tf_op jit(solution)/shard_map/ppermute | solution.py:280
  55.2 6.0 %collective-permute-start.2 = (bf16[384,2048]{1,0:T(8,128)(2,1)}, bf16[384,2048]{1,0:T(8,128)(2,1)}, u32[]{:S(2)}, u32[]{:S(2)}) collective-permute-start(bf16[384,2048]{1,0:T(8,128)(2,1)} %bitcast.19), channel_id=1, source_target_pairs={{0,1},{1,0},{2,3},{3,2},{4,5},{5,4},{6,7},{7,6},{8,9},{9,8},{10,11... | collective-permute-start | bytes 4718600 | tf_op jit(solution)/shard_map/ppermute | solution.py:280
  57.6 1.2 copy-start.3
  58.8 1.1 copy-start.4
  99.5 8.8 %copy-start.2 = (f32[128,2]{0,1:T(2,128)S(1)}, f32[128,2]{0,1:T(2,128)}, u32[]{:S(2)}) copy-start(f32[128,2]{0,1:T(2,128)} %param.12) | copy-start | bytes 3076
  99.5 50.5 %all-to-all-start.2 = ((bf16[64,8,1536]{2,1,0:T(8,128)(2,1)}), bf16[64,8,1536]{2,1,0:T(8,128)(2,1)S(1)}, u32[]{:S(2)}, u32[]{:S(2)}) async-start(bf16[64,8,1536]{2,1,0:T(8,128)(2,1)} %bitcast.8), calls=%async_computation.2 | async-start | bytes 3145728 | tf_op jit(solution)/shard_map/all_to_all | solution.py:293

commit v4 on v3

--- a/solution.py
+++ b/solution.py
@@ -62,10 +62,9 @@
     finish(start((out_ref, out_hbm, sems.at[3])))
 
 
-def dispatch_kernel(routes_ref, rows_ref, out_hbm, out_ref, sems):
-    length, width = rows_ref.shape
-    experts = out_ref.shape[0] // GROUP
-    block = width // (BLOCKS + 1)
+def slots_kernel(routes_ref, picks_ref):
+    length = routes_ref.shape[1]
+    experts = picks_ref.shape[0] // GROUP
     expert = iota((experts, length), 0)
     named = (expert == routes_ref[0:1, :]) | (expert == routes_ref[1:2, :])
     earlier = (iota((length, length), 0) < iota((length, length), 1)).astype(F32).astype(BF16)
@@ -77,12 +76,21 @@
         hit = position == wanted.astype(F32)
         return hit.astype(F32).reshape(experts * GROUP, length).astype(BF16)
 
-    main = placed(jnp.where(k < CAP, k, -2))
+    picks_ref[:, :length] = placed(jnp.where(k < CAP, k, -2))
+    for j in range(BLOCKS):
+        tail = placed(jnp.where(k == CAP, j, jnp.where(k == CAP + 1, BLOCKS + j, -2)))
+        picks_ref[:, (j + 1) * length : (j + 2) * length] = tail
+
+
+def dispatch_kernel(picks_ref, rows_ref, out_hbm, out_ref, sems):
+    length, width = rows_ref.shape
+    block = width // (BLOCKS + 1)
+    main = picks_ref[:, :length]
     tail_rows = rows_ref[:, BLOCKS * block :]
     copies = []
     for j in range(BLOCKS):
         at = slice(j * block, (j + 1) * block)
-        tail = placed(jnp.where(k == CAP, j, jnp.where(k == CAP + 1, BLOCKS + j, -2)))
+        tail = picks_ref[:, (j + 1) * length : (j + 2) * length]
         both = jnp.concatenate([main, tail], axis=1)
         source = jnp.concatenate([rows_ref[:, at], tail_rows], axis=0)
         out_ref[:, at] = dot(both, source).astype(BF16)
@@ -228,10 +236,18 @@
     )
 
 
-def dispatch(routes_t, sequence, slots, wide):
-    length = sequence.shape[0]
+def find_slots(routes_t, slots):
+    return pl.pallas_call(
+        slots_kernel,
+        out_shape=jax.ShapeDtypeStruct((slots, (BLOCKS + 1) * routes_t.shape[1]), BF16),
+        compiler_params=pltpu.CompilerParams(vmem_limit_bytes=16 << 20),
+    )(routes_t)
+
+
+def dispatch(picks, sequence, wide):
+    length, slots = sequence.shape[0], picks.shape[0]
     return call(
-        dispatch_kernel, (slots, wide), routes_t, sequence,
+        dispatch_kernel, (slots, wide), picks, sequence,
         flops=4 * slots * length * wide,
         scratch=[((slots, wide), BF16)], sems=BLOCKS, here=(0, 1),
     )
@@ -252,9 +268,8 @@
     )
 
 
-def combine(routes, route_scale, returned, width):
-    length, slots = routes.shape[0], returned.shape[0]
-    at, share = pl.pallas_call(
+def find_places(routes, route_scale):
+    return pl.pallas_call(
         places_kernel,
         out_shape=[
             jax.ShapeDtypeStruct(routes.shape, I32),
@@ -262,6 +277,10 @@
         ],
         compiler_params=pltpu.CompilerParams(vmem_limit_bytes=16 << 20),
     )(routes, route_scale)
+
+
+def combine(at, share, returned, width):
+    length, slots = at.shape[0], returned.shape[0]
     return call(
         combine_kernel, (length, width), at, share, returned,
         flops=8 * length * slots * returned.shape[1],
@@ -287,7 +306,8 @@
         concat_axis=0,
         tiled=True,
     )
-    buffer = dispatch(routes.T, arrived.reshape(length, width), slots, wide)
+    picks = find_slots(routes.T, slots)
+    buffer = dispatch(picks, arrived.reshape(length, width), wide)
 
     def exchange(x):
         y = lax.all_to_all(
@@ -295,8 +315,10 @@
         )
         return y.reshape(slots, wide)
 
-    returned = exchange(run_expert(exchange(buffer), own, other))
-    return combine(routes, route_scale, returned, width)
+    received = exchange(buffer)
+    received, places = lax.optimization_barrier((received, find_places(routes, route_scale)))
+    returned = exchange(run_expert(received, own, other))
+    return combine(*places, returned, width)
 
 
 def solution(mesh):

time: 152 us -> 151 us (level)
  blocking collectives: 22.9 us -> 50.2 us
  waiting for transfers between devices: 74.2 us -> 49.3 us
  starting transfers between devices: 39.5 us -> 37.7 us
    all_to_all x2 -> x1, waiting for transfers between devices: 71.8 us -> 33.6 us  [exchange(): lax.all_to_all(x.reshape(experts, GROUP, wide), 'expert', split_axis=0, c...]
    all_to_all x1, blocking collectives: 22.9 us -> 50.2 us  [exchange(): lax.all_to_all(x.reshape(experts, GROUP, wide), 'expert', split_axis=0, c...]
    all_to_all x0 -> x1, waiting for transfers between devices: none -> 15.7 us  [local(): lax.all_to_all(outgoing.reshape(owners, length // owners, width), ('dp',...]
    all_to_all x2 -> x1, starting transfers between devices: 32.1 us -> 23.4 us  [exchange(): lax.all_to_all(x.reshape(experts, GROUP, wide), 'expert', split_axis=0, c...]
    all_to_all x0 -> x1, starting transfers between devices: none -> 6.88 us  [local(): lax.all_to_all(outgoing.reshape(owners, length // owners, width), ('dp',...]
    ppermute x3, waiting for transfers between devices: 2.37 us -> 0.01 us  [local(): other = [lax.ppermute(w, 'mp', [(0, 1), (1, 0)]) for w in own]]
  transfers between devices with their start and end apart: 5 -> 5, of which waited for: 4 -> 2; matrix products, arithmetic and copies ran while one was open for 0% -> 0% of each run, Pallas kernels for 0% -> 0%
where the time goes in v4:
time: 151 us
  blocking collectives  50.2 us (33%)
  waiting for transfers between devices  49.3 us (33%)
  starting transfers between devices  37.7 us (25%)
  Pallas kernels  13.2 us (9%)
    all_to_all x1, blocking collectives, exchange(): lax.all_to_all(x.reshape(experts, GROUP, wide), 'expert', split_axis=0, c...  50.2 us
    all_to_all x1, waiting for transfers between devices, exchange(): lax.all_to_all(x.reshape(experts, GROUP, wide), 'expert', split_axis=0, c...  33.6 us
    all_to_all x1, starting transfers between devices, exchange(): lax.all_to_all(x.reshape(experts, GROUP, wide), 'expert', split_axis=0, c...  23.4 us
    all_to_all x1, waiting for transfers between devices, local(): lax.all_to_all(outgoing.reshape(owners, length // owners, width), ('dp',...  15.7 us
    pallas_call x4, Pallas kernels, call(): pl.pallas_call(kernel, out_shape=jax.ShapeDtypeStruct(out, BF16), in_spec...  12.6 us
    ppermute x3, starting transfers between devices, local(): other = [lax.ppermute(w, 'mp', [(0, 1), (1, 0)]) for w in own]  7.39 us
    all_to_all x1, starting transfers between devices, local(): lax.all_to_all(outgoing.reshape(owners, length // owners, width), ('dp',...  6.88 us
  transfers between devices with their start and end apart: 5, of which 2 were waited for; matrix products, arithmetic and copies ran while one was open for 0% of the time, Pallas kernels for 0%

profile of v4, /device:TPU:16, one launch (start us, length us, event | category | flops | bytes accessed | tf_op | source)
XLA Modules:
  0.0 150.8 jit_solution(11253953418179392793)
XLA Ops:
  0.0 0.0 copy-start
  0.0 2.1 %shard_map.83 = bf16[128,2048]{1,0:T(8,128)(2,1)} custom-call(s32[1,16]{1,0:T(1,128)} %counts_hbm.1, s32[1,16]{1,0:T(1,128)} %owner_hbm.1, bf16[80,2048]{1,0:T(8,128)(2,1)} %rows_hbm.1), custom_call_target="tpu_custom_call" | custom-call | flops 41943040 | bytes 852096 | tf_op jit(solution)/shard_map/pallas_call | solution.py:216
  2.1 6.9 %all-to-all-start = ((bf16[16,8,2048]{2,1,0:T(8,128)(2,1)}), bf16[16,8,2048]{2,1,0:T(8,128)(2,1)S(1)}, u32[]{:S(2)}, u32[]{:S(2)}) async-start(bf16[16,8,2048]{2,1,0:T(8,128)(2,1)} %bitcast.17), calls=%async_computation | async-start | bytes 1048576 | tf_op jit(solution)/shard_map/all_to_all | solution.py:302
  9.0 0.0 copy-done
  9.0 0.3 shard_map.82.picks_ref
  9.3 15.7 %all-to-all-done = bf16[16,8,2048]{2,1,0:T(8,128)(2,1)S(1)} async-done(((bf16[16,8,2048]{2,1,0:T(8,128)(2,1)}), bf16[16,8,2048]{2,1,0:T(8,128)(2,1)S(1)}, u32[]{:S(2)}, u32[]{:S(2)}) %all-to-all-start) | async-done | bytes 524320 | tf_op jit(solution)/shard_map/all_to_all | solution.py:302
  25.0 1.5 shard_map.84
  26.5 0.0 copy-start.1
  26.5 0.0 copy-start.2
  26.6 23.4 %all-to-all-start.1 = ((bf16[64,8,1536]{2,1,0:T(8,128)(2,1)}), bf16[64,8,1536]{2,1,0:T(8,128)(2,1)S(1)}, u32[]{:S(2)}, u32[]{:S(2)}) async-start(bf16[64,8,1536]{2,1,0:T(8,128)(2,1)} %bitcast.3), calls=%async_computation.1 | async-start | bytes 3145728 | tf_op jit(solution)/shard_map/all_to_all | solution.py:313
  50.0 0.0 copy-done.1
  50.0 3.1 %collective-permute-start = (bf16[2048,384]{1,0:T(8,128)(2,1)S(1)}, bf16[2048,384]{1,0:T(8,128)(2,1)}, u32[]{:S(2)}, u32[]{:S(2)}) collective-permute-start(bf16[2048,384]{1,0:T(8,128)(2,1)S(1)} %bitcast.15), channel_id=1, source_target_pairs={{0,1},{1,0},{2,3},{3,2},{4,5},{5,4},{6,7},{7,6},{8,9},{9,8},{10,11... | collective-permute-start | bytes 4718600 | tf_op jit(solution)/shard_map/ppermute | solution.py:299
  53.1 1.9 %collective-permute-start.1 = (bf16[2048,384]{1,0:T(8,128)(2,1)}, bf16[2048,384]{1,0:T(8,128)(2,1)}, u32[]{:S(2)}, u32[]{:S(2)}) collective-permute-start(bf16[2048,384]{1,0:T(8,128)(2,1)} %bitcast.18), channel_id=1, source_target_pairs={{0,1},{1,0},{2,3},{3,2},{4,5},{5,4},{6,7},{7,6},{8,9},{9,8},{10,11... | collective-permute-start | bytes 4718600 | tf_op jit(solution)/shard_map/ppermute | solution.py:299
  55.0 2.4 %collective-permute-start.2 = (bf16[384,2048]{1,0:T(8,128)(2,1)}, bf16[384,2048]{1,0:T(8,128)(2,1)}, u32[]{:S(2)}, u32[]{:S(2)}) collective-permute-start(bf16[384,2048]{1,0:T(8,128)(2,1)} %bitcast.20), channel_id=1, source_target_pairs={{0,1},{1,0},{2,3},{3,2},{4,5},{5,4},{6,7},{7,6},{8,9},{9,8},{10,11... | collective-permute-start | bytes 4718600 | tf_op jit(solution)/shard_map/ppermute | solution.py:299
  57.4 0.1 copy.9.routes_ref
  57.5 0.0 copy-done.2
  57.5 0.1 copy.10.scale_ref
  57.6 0.3 shard_map.85
  58.0 33.6 %all-to-all-done.1 = bf16[64,8,1536]{2,1,0:T(8,128)(2,1)S(1)} async-done(((bf16[64,8,1536]{2,1,0:T(8,128)(2,1)}), bf16[64,8,1536]{2,1,0:T(8,128)(2,1)S(1)}, u32[]{:S(2)}, u32[]{:S(2)}) %all-to-all-start.1) | async-done | bytes 1572896 | tf_op jit(solution)/shard_map/all_to_all | solution.py:313
  91.6 0.0 collective-permute-done.gate_b
  91.6 0.0 collective-permute-done.1.up_b
  91.6 0.0 collective-permute-done.2.down_b
  91.6 7.3 %shard_map.86 = bf16[512,1536]{1,0:T(8,128)(2,1)S(1)} custom-call(bf16[512,1536]{1,0:T(8,128)(2,1)S(1)} %bitcast.11, bf16[2048,384]{1,0:T(8,128)(2,1)S(1)} %bitcast.16, bf16[2048,384]{1,0:T(8,128)(2,1)} %bitcast.19, bf16[384,2048]{1,0:T(8,128)(2,1)} %bitcast.21, bf16[2048,384]{1,0:T(8,128)(2,1)} %collective-permute-done.gate_b, ...), custom_call_target="tpu_custom_call" | custom-call | flops 4831838208 | bytes 12582912 | tf_op jit(solution)/shard_map/pallas_call | solution.py:216
  98.9 50.2 %all_to_all.15 = bf16[64,8,1536]{2,1,0:T(8,128)(2,1)S(1)} all-to-all(bf16[64,8,1536]{2,1,0:T(8,128)(2,1)S(1)} %bitcast.12), channel_id=1, replica_groups=mesh['dp'=8,'expert'=64,'mp'=2] {'expert'}, dimensions={0} | all-to-all | bytes 3145728 | tf_op jit(solution)/shard_map/all_to_all | solution.py:313
  149.1 1.7 %shard_map.87 = bf16[128,2048]{1,0:T(8,128)(2,1)} custom-call(s32[128,2]{1,0:T(8,128)S(1)} %get-tuple-element.12.at_ref, f32[128,2]{1,0:T(8,128)S(1)} %get-tuple-element.13.share_ref, bf16[512,1536]{1,0:T(8,128)(2,1)S(1)} %bitcast.13), custom_call_target="tpu_custom_call" | custom-call | flops 805306368 | bytes 2099200 | tf_op jit(solution)/shard_map/pallas_call | solution.py:216
Async XLA Ops:
  0.0 9.0 %copy-start = (s32[128,2]{0,1:T(2,128)S(1)}, s32[128,2]{0,1:T(2,128)}, u32[]{:S(2)}) copy-start(s32[128,2]{0,1:T(2,128)} %param.11) | copy-start | bytes 3076
  2.1 22.9 %all-to-all-start = ((bf16[16,8,2048]{2,1,0:T(8,128)(2,1)}), bf16[16,8,2048]{2,1,0:T(8,128)(2,1)S(1)}, u32[]{:S(2)}, u32[]{:S(2)}) async-start(bf16[16,8,2048]{2,1,0:T(8,128)(2,1)} %bitcast.17), calls=%async_computation | async-start | bytes 1048576 | tf_op jit(solution)/shard_map/all_to_all | solution.py:302
  26.5 23.5 %copy-start.1 = (bf16[1,2048,384]{2,1,0:T(8,128)(2,1)S(1)}, bf16[1,2048,384]{2,1,0:T(8,128)(2,1)}, u32[]{:S(2)}) copy-start(bf16[1,2048,384]{2,1,0:T(8,128)(2,1)} %param.13) | copy-start | bytes 4718596
  26.5 31.0 %copy-start.2 = (f32[128,2]{0,1:T(2,128)S(1)}, f32[128,2]{0,1:T(2,128)}, u32[]{:S(2)}) copy-start(f32[128,2]{0,1:T(2,128)} %param.12) | copy-start | bytes 3076
  26.6 65.0 %all-to-all-start.1 = ((bf16[64,8,1536]{2,1,0:T(8,128)(2,1)}), bf16[64,8,1536]{2,1,0:T(8,128)(2,1)S(1)}, u32[]{:S(2)}, u32[]{:S(2)}) async-start(bf16[64,8,1536]{2,1,0:T(8,128)(2,1)} %bitcast.3), calls=%async_computation.1 | async-start | bytes 3145728 | tf_op jit(solution)/shard_map/all_to_all | solution.py:313
  50.0 41.6 %collective-permute-start = (bf16[2048,384]{1,0:T(8,128)(2,1)S(1)}, bf16[2048,384]{1,0:T(8,128)(2,1)}, u32[]{:S(2)}, u32[]{:S(2)}) collective-permute-start(bf16[2048,384]{1,0:T(8,128)(2,1)S(1)} %bitcast.15), channel_id=1, source_target_pairs={{0,1},{1,0},{2,3},{3,2},{4,5},{5,4},{6,7},{7,6},{8,9},{9,8},{10,11... | collective-permute-start | bytes 4718600 | tf_op jit(solution)/shard_map/ppermute | solution.py:299
  53.1 38.5 %collective-permute-start.1 = (bf16[2048,384]{1,0:T(8,128)(2,1)}, bf16[2048,384]{1,0:T(8,128)(2,1)}, u32[]{:S(2)}, u32[]{:S(2)}) collective-permute-start(bf16[2048,384]{1,0:T(8,128)(2,1)} %bitcast.18), channel_id=1, source_target_pairs={{0,1},{1,0},{2,3},{3,2},{4,5},{5,4},{6,7},{7,6},{8,9},{9,8},{10,11... | collective-permute-start | bytes 4718600 | tf_op jit(solution)/shard_map/ppermute | solution.py:299
  55.0 36.6 %collective-permute-start.2 = (bf16[384,2048]{1,0:T(8,128)(2,1)}, bf16[384,2048]{1,0:T(8,128)(2,1)}, u32[]{:S(2)}, u32[]{:S(2)}) collective-permute-start(bf16[384,2048]{1,0:T(8,128)(2,1)} %bitcast.20), channel_id=1, source_target_pairs={{0,1},{1,0},{2,3},{3,2},{4,5},{5,4},{6,7},{7,6},{8,9},{9,8},{10,11... | collective-permute-start | bytes 4718600 | tf_op jit(solution)/shard_map/ppermute | solution.py:299

commit v5 on v4

--- a/solution.py
+++ b/solution.py
@@ -99,8 +99,8 @@
 
 
 def expert_kernel(
-    x_ref, gate_a, up_a, down_a, gate_b, up_b, down_b, out_hbm,
-    gate_ref, up_ref, down_ref, rows_ref, act_ref, out_ref, sems,
+    x_ref, gate_a, up_a, down_a, gate_b, up_b, down_b, out_ref,
+    gate_ref, up_ref, down_ref, rows_ref, act_ref, sems,
 ):
     chunk_rows, wide = x_ref.shape
     block = wide // BLOCKS
@@ -150,7 +150,6 @@
     act_ref[...] = (gate / (1.0 + jnp.exp(-gate)) * up).astype(BF16)
     finish(downs)
     last = dot(act_ref[...], down_ref[:, wide:]).astype(BF16)
-    copies = []
     for j in range(BLOCKS):
         at = slice(j * block, (j + 1) * block)
         result = dot(act_ref[...], down_ref[:, at]).astype(BF16)
@@ -159,8 +158,6 @@
             tails = [source + (j + k) * chunks for k in (0, BLOCKS)]
             both = [result[source : source + packed]] + [last[i : i + chunks] for i in tails]
             out_ref[target, at] = dot(spread, jnp.concatenate(both, axis=0)).astype(BF16)
-        copies += start((out_ref.at[:, at], out_hbm.at[:, at], sems.at[4 * cuts + 2 + j]))
-    finish(copies)
 
 
 def places_kernel(routes_ref, scale_ref, at_ref, share_ref):
@@ -211,13 +208,13 @@
     finish(copies + start((out_ref.at[:, at], out_hbm.at[:, at], sems.at[BLOCKS])))
 
 
-def call(kernel, out, *args, flops, scratch, sems, here=(), limit=32 << 20):
+def call(kernel, out, *args, flops, scratch, sems, here=(), out_here=False, limit=32 << 20):
     moved = sum(a.size * a.dtype.itemsize for a in args) + out[0] * out[1] * 2
     return pl.pallas_call(
         kernel,
         out_shape=jax.ShapeDtypeStruct(out, BF16),
         in_specs=[VMEM if i in here else ANY for i in range(len(args))],
-        out_specs=ANY,
+        out_specs=VMEM if out_here else ANY,
         scratch_shapes=[pltpu.VMEM(*s) for s in scratch] + [pltpu.SemaphoreType.DMA((sems,))],
         compiler_params=pltpu.CompilerParams(vmem_limit_bytes=limit),
         cost_estimate=pl.CostEstimate(flops=flops, bytes_accessed=moved, transcendentals=0),
@@ -262,9 +259,9 @@
         flops=12 * slots * width * half,
         scratch=[
             ((width, 2 * half), BF16), ((width, 2 * half), BF16), ((2 * half, width), BF16),
-            ((rows, width), BF16), ((rows, 2 * half), BF16), ((slots, wide), BF16),
+            ((rows, width), BF16), ((rows, 2 * half), BF16),
         ],
-        sems=18 + BLOCKS, here=(0,), limit=48 << 20,
+        sems=18, here=(0,), out_here=True, limit=48 << 20,
     )
 
 

time: 151 us -> 151 us (level)
  no operation moved by 1% of the time
where the time goes in v5:
time: 151 us; the launch traced here: 150 us
  blocking collectives  50.2 us (33%)
  waiting for transfers between devices  49.3 us (33%)
  starting transfers between devices  37.7 us (25%)
  Pallas kernels  12.8 us (8%)
    all_to_all x1, blocking collectives, exchange(): lax.all_to_all(x.reshape(experts, GROUP, wide), 'expert', split_axis=0, c...  50.2 us
    all_to_all x1, waiting for transfers between devices, exchange(): lax.all_to_all(x.reshape(experts, GROUP, wide), 'expert', split_axis=0, c...  33.6 us
    all_to_all x1, starting transfers between devices, exchange(): lax.all_to_all(x.reshape(experts, GROUP, wide), 'expert', split_axis=0, c...  23.4 us
    all_to_all x1, waiting for transfers between devices, local(): lax.all_to_all(outgoing.reshape(owners, length // owners, width), ('dp',...  15.7 us
    pallas_call x4, Pallas kernels, call(): pl.pallas_call(kernel, out_shape=jax.ShapeDtypeStruct(out, BF16), in_spec...  12.2 us
    ppermute x3, starting transfers between devices, local(): other = [lax.ppermute(w, 'mp', [(0, 1), (1, 0)]) for w in own]  7.39 us
    all_to_all x1, starting transfers between devices, local(): lax.all_to_all(outgoing.reshape(owners, length // owners, width), ('dp',...  6.88 us
  transfers between devices with their start and end apart: 5, of which 2 were waited for; matrix products, arithmetic and copies ran while one was open for 0% of the time, Pallas kernels for 0%

profile of v5, /device:TPU:16, one launch (start us, length us, event | category | flops | bytes accessed | tf_op | source)
XLA Modules:
  0.0 150.4 jit_solution(6698682793814896413)
XLA Ops:
  0.0 0.0 copy-start
  0.0 2.1 %shard_map.83 = bf16[128,2048]{1,0:T(8,128)(2,1)} custom-call(s32[1,16]{1,0:T(1,128)} %counts_hbm.1, s32[1,16]{1,0:T(1,128)} %owner_hbm.1, bf16[80,2048]{1,0:T(8,128)(2,1)} %rows_hbm.1), custom_call_target="tpu_custom_call" | custom-call | flops 41943040 | bytes 852096 | tf_op jit(solution)/shard_map/pallas_call | solution.py:213
  2.1 6.9 %all-to-all-start = ((bf16[16,8,2048]{2,1,0:T(8,128)(2,1)}), bf16[16,8,2048]{2,1,0:T(8,128)(2,1)S(1)}, u32[]{:S(2)}, u32[]{:S(2)}) async-start(bf16[16,8,2048]{2,1,0:T(8,128)(2,1)} %bitcast.17), calls=%async_computation | async-start | bytes 1048576 | tf_op jit(solution)/shard_map/all_to_all | solution.py:299
  9.0 0.0 copy-done
  9.0 0.3 shard_map.82.picks_ref
  9.3 15.7 %all-to-all-done = bf16[16,8,2048]{2,1,0:T(8,128)(2,1)S(1)} async-done(((bf16[16,8,2048]{2,1,0:T(8,128)(2,1)}), bf16[16,8,2048]{2,1,0:T(8,128)(2,1)S(1)}, u32[]{:S(2)}, u32[]{:S(2)}) %all-to-all-start) | async-done | bytes 524320 | tf_op jit(solution)/shard_map/all_to_all | solution.py:299
  25.0 1.5 shard_map.84
  26.5 0.0 copy-start.1
  26.5 0.0 copy-start.2
  26.6 23.4 %all-to-all-start.1 = ((bf16[64,8,1536]{2,1,0:T(8,128)(2,1)}), bf16[64,8,1536]{2,1,0:T(8,128)(2,1)S(1)}, u32[]{:S(2)}, u32[]{:S(2)}) async-start(bf16[64,8,1536]{2,1,0:T(8,128)(2,1)} %bitcast.3), calls=%async_computation.1 | async-start | bytes 3145728 | tf_op jit(solution)/shard_map/all_to_all | solution.py:310
  50.0 0.0 copy-done.1
  50.0 3.1 %collective-permute-start = (bf16[2048,384]{1,0:T(8,128)(2,1)S(1)}, bf16[2048,384]{1,0:T(8,128)(2,1)}, u32[]{:S(2)}, u32[]{:S(2)}) collective-permute-start(bf16[2048,384]{1,0:T(8,128)(2,1)S(1)} %bitcast.15), channel_id=1, source_target_pairs={{0,1},{1,0},{2,3},{3,2},{4,5},{5,4},{6,7},{7,6},{8,9},{9,8},{10,11... | collective-permute-start | bytes 4718600 | tf_op jit(solution)/shard_map/ppermute | solution.py:296
  53.1 1.9 %collective-permute-start.1 = (bf16[2048,384]{1,0:T(8,128)(2,1)}, bf16[2048,384]{1,0:T(8,128)(2,1)}, u32[]{:S(2)}, u32[]{:S(2)}) collective-permute-start(bf16[2048,384]{1,0:T(8,128)(2,1)} %bitcast.18), channel_id=1, source_target_pairs={{0,1},{1,0},{2,3},{3,2},{4,5},{5,4},{6,7},{7,6},{8,9},{9,8},{10,11... | collective-permute-start | bytes 4718600 | tf_op jit(solution)/shard_map/ppermute | solution.py:296
  55.0 2.4 %collective-permute-start.2 = (bf16[384,2048]{1,0:T(8,128)(2,1)}, bf16[384,2048]{1,0:T(8,128)(2,1)}, u32[]{:S(2)}, u32[]{:S(2)}) collective-permute-start(bf16[384,2048]{1,0:T(8,128)(2,1)} %bitcast.20), channel_id=1, source_target_pairs={{0,1},{1,0},{2,3},{3,2},{4,5},{5,4},{6,7},{7,6},{8,9},{9,8},{10,11... | collective-permute-start | bytes 4718600 | tf_op jit(solution)/shard_map/ppermute | solution.py:296
  57.4 0.1 copy.9.routes_ref
  57.5 0.0 copy-done.2
  57.5 0.1 copy.10.scale_ref
  57.6 0.3 shard_map.85
  58.0 33.6 %all-to-all-done.1 = bf16[64,8,1536]{2,1,0:T(8,128)(2,1)S(1)} async-done(((bf16[64,8,1536]{2,1,0:T(8,128)(2,1)}), bf16[64,8,1536]{2,1,0:T(8,128)(2,1)S(1)}, u32[]{:S(2)}, u32[]{:S(2)}) %all-to-all-start.1) | async-done | bytes 1572896 | tf_op jit(solution)/shard_map/all_to_all | solution.py:310
  91.6 0.0 collective-permute-done.gate_b
  91.6 0.0 collective-permute-done.1.up_b
  91.6 0.0 collective-permute-done.2.down_b
  91.6 6.8 %shard_map.86 = bf16[512,1536]{1,0:T(8,128)(2,1)S(1)} custom-call(bf16[512,1536]{1,0:T(8,128)(2,1)S(1)} %bitcast.11, bf16[2048,384]{1,0:T(8,128)(2,1)S(1)} %bitcast.16, bf16[2048,384]{1,0:T(8,128)(2,1)} %bitcast.19, bf16[384,2048]{1,0:T(8,128)(2,1)} %bitcast.21, bf16[2048,384]{1,0:T(8,128)(2,1)} %collective-permute-done.gate_b, ...), custom_call_target="tpu_custom_call" | custom-call | flops 4831838208 | bytes 12582912 | tf_op jit(solution)/shard_map/pallas_call | solution.py:213
  98.4 50.2 %all_to_all.15 = bf16[64,8,1536]{2,1,0:T(8,128)(2,1)S(1)} all-to-all(bf16[64,8,1536]{2,1,0:T(8,128)(2,1)S(1)} %bitcast.12), channel_id=1, replica_groups=mesh['dp'=8,'expert'=64,'mp'=2] {'expert'}, dimensions={0} | all-to-all | bytes 3145728 | tf_op jit(solution)/shard_map/all_to_all | solution.py:310
  148.6 1.7 %shard_map.87 = bf16[128,2048]{1,0:T(8,128)(2,1)} custom-call(s32[128,2]{1,0:T(8,128)S(1)} %get-tuple-element.12.at_ref, f32[128,2]{1,0:T(8,128)S(1)} %get-tuple-element.13.share_ref, bf16[512,1536]{1,0:T(8,128)(2,1)S(1)} %bitcast.13), custom_call_target="tpu_custom_call" | custom-call | flops 805306368 | bytes 2099200 | tf_op jit(solution)/shard_map/pallas_call | solution.py:213
Async XLA Ops:
  0.0 9.0 %copy-start = (s32[128,2]{0,1:T(2,128)S(1)}, s32[128,2]{0,1:T(2,128)}, u32[]{:S(2)}) copy-start(s32[128,2]{0,1:T(2,128)} %param.11) | copy-start | bytes 3076
  2.1 22.9 %all-to-all-start = ((bf16[16,8,2048]{2,1,0:T(8,128)(2,1)}), bf16[16,8,2048]{2,1,0:T(8,128)(2,1)S(1)}, u32[]{:S(2)}, u32[]{:S(2)}) async-start(bf16[16,8,2048]{2,1,0:T(8,128)(2,1)} %bitcast.17), calls=%async_computation | async-start | bytes 1048576 | tf_op jit(solution)/shard_map/all_to_all | solution.py:299
  26.5 23.5 %copy-start.1 = (bf16[1,2048,384]{2,1,0:T(8,128)(2,1)S(1)}, bf16[1,2048,384]{2,1,0:T(8,128)(2,1)}, u32[]{:S(2)}) copy-start(bf16[1,2048,384]{2,1,0:T(8,128)(2,1)} %param.13) | copy-start | bytes 4718596
  26.5 31.0 %copy-start.2 = (f32[128,2]{0,1:T(2,128)S(1)}, f32[128,2]{0,1:T(2,128)}, u32[]{:S(2)}) copy-start(f32[128,2]{0,1:T(2,128)} %param.12) | copy-start | bytes 3076
  26.6 65.0 %all-to-all-start.1 = ((bf16[64,8,1536]{2,1,0:T(8,128)(2,1)}), bf16[64,8,1536]{2,1,0:T(8,128)(2,1)S(1)}, u32[]{:S(2)}, u32[]{:S(2)}) async-start(bf16[64,8,1536]{2,1,0:T(8,128)(2,1)} %bitcast.3), calls=%async_computation.1 | async-start | bytes 3145728 | tf_op jit(solution)/shard_map/all_to_all | solution.py:310
  50.0 41.6 %collective-permute-start = (bf16[2048,384]{1,0:T(8,128)(2,1)S(1)}, bf16[2048,384]{1,0:T(8,128)(2,1)}, u32[]{:S(2)}, u32[]{:S(2)}) collective-permute-start(bf16[2048,384]{1,0:T(8,128)(2,1)S(1)} %bitcast.15), channel_id=1, source_target_pairs={{0,1},{1,0},{2,3},{3,2},{4,5},{5,4},{6,7},{7,6},{8,9},{9,8},{10,11... | collective-permute-start | bytes 4718600 | tf_op jit(solution)/shard_map/ppermute | solution.py:296
  53.1 38.5 %collective-permute-start.1 = (bf16[2048,384]{1,0:T(8,128)(2,1)}, bf16[2048,384]{1,0:T(8,128)(2,1)}, u32[]{:S(2)}, u32[]{:S(2)}) collective-permute-start(bf16[2048,384]{1,0:T(8,128)(2,1)} %bitcast.18), channel_id=1, source_target_pairs={{0,1},{1,0},{2,3},{3,2},{4,5},{5,4},{6,7},{7,6},{8,9},{9,8},{10,11... | collective-permute-start | bytes 4718600 | tf_op jit(solution)/shard_map/ppermute | solution.py:296
  55.0 36.6 %collective-permute-start.2 = (bf16[384,2048]{1,0:T(8,128)(2,1)}, bf16[384,2048]{1,0:T(8,128)(2,1)}, u32[]{:S(2)}, u32[]{:S(2)}) collective-permute-start(bf16[384,2048]{1,0:T(8,128)(2,1)} %bitcast.20), channel_id=1, source_target_pairs={{0,1},{1,0},{2,3},{3,2},{4,5},{5,4},{6,7},{7,6},{8,9},{9,8},{10,11... | collective-permute-start | bytes 4718600 | tf_op jit(solution)/shard_map/ppermute | solution.py:296
